TPU v7x, 32 devices: a whole 2x2x4 slice. The times are simulated.
32 devices in a mesh: leaf: 8 (over z, x), col: 4 (over y, core).
Axes of the slice: x: 2, y: 2, z: 4, core: 2. Of those that a mesh axis runs over, the one named last changes fastest.
Arguments:
- points: float32 [8192, 128], P(('leaf', 'col')), may hold values from -6 to 6
- coefs: float32 [8192, 512], P(('leaf', 'col')), may hold values from -6 to 6
- targets: float32 [8192, 512], P(('leaf', 'col')), may hold values from -6 to 6
- ridge: float32 [1], replicated, may hold values from 0.5 to 2
- tile_mask: int32 [8, 5], P('leaf'), may hold values from 0 to 1, as said below
- cluster_perm: int32 [8, 1024], P('leaf'), may hold values from 0 to 1023, each once within a row
- leaf_map: int32 [8], replicated, may hold values from 0 to 7, as said below
- leaf_inverse: float32 [8, 1024, 1024], P('leaf'), may hold values from -0.25 to 1.3
- leaf_basis: float32 [8, 1024, 256], P('leaf'), may hold values from -0.1875 to 0.1875
- node_inverse: float32 [8, 320, 1024], P('leaf'), may hold values from -0.25 to 1.3
- node_transfer: float32 [8, 320, 256], P('leaf'), may hold values from -0.1875 to 0.1875
Outputs:
- residual: float32 [8192, 512], P(('leaf', 'col'))
- new_coef: float32 [8192, 512], P(('leaf', 'col'))
Inputs may be any that keep to these rules, and one draw needn't show every extreme that they name: `tile_mask`: entry k of row i is 1 when block i has a nonzero tile with block i + k - 2; entry 2 is always 1, entries naming a block outside 0 .. 7 are 0, and some row lists all 5 tiles. `cluster_perm`: each row is a permutation of 0 .. 1023. `leaf_map`: a permutation of 0 .. 7 that sends the tree leaves 4 n .. 4 n + 3 to the blocks 4 n .. 4 n + 3.
All inputs are finite; a program needn't handle non-finite values.
Results may differ from a plain program's by a relative error of at most 0.0003.
Values sent between devices are 32-bit elements; how exact they have to be, the bound alone decides.
A program may use at most 128 MiB of HBM per device.

v0:
```python
import jax
import jax.numpy as jnp
from jax import lax
from jax.sharding import PartitionSpec as P

highest = lax.Precision.HIGHEST


def from_partner(block, axis, bit):
    count = lax.axis_size(axis)
    route = []
    for low in range(count):
        high = low | 1 << bit
        if high != low and high < count:
            route += [(low, high), (high, low)]
    return lax.ppermute(block, axis, route)


def shifted(value, axis, steps):
    count = lax.axis_size(axis)
    initial, last = (max(0, -steps), min(count, count - steps))
    return lax.ppermute(value, axis, [(source, source + steps) for source in range(initial, last)])


def kernel_tile(row_points, row_squares, column_points, column_squares):
    inner_products = jnp.einsum("pf,qf->pq", row_points, column_points, precision=highest)
    distance = row_squares[:, None] + column_squares[None, :] - 2.0 * inner_products
    return jnp.exp(distance * (-2.0 / row_points.shape[1]))


def tree_levels(remaining, rank_size):
    levels = []
    covered = 1
    height = 1
    offset = 0
    while remaining > 1:
        children = 4 if remaining % 4 == 0 else remaining
        covered = covered * children
        remaining = remaining // children
        slice_count = children * rank_size // covered
        levels.append((height, children, covered, offset, slice_count))
        offset = offset + slice_count
        height = height + 1
    return levels


def pair_order(mine, partner, leaf_pos, bit):
    upper_side = leaf_pos // (1 << bit) % 2 == 1
    first_half = jnp.where(upper_side, partner, mine)
    second_half = jnp.where(upper_side, mine, partner)
    return jnp.concatenate([first_half, second_half], axis=0)


def gather_up(values_in, low_bit, high_bit, leaf_pos):
    for bit in range(low_bit, high_bit):
        partner = from_partner(values_in, "leaf", bit)
        values_in = pair_order(values_in, partner, leaf_pos, bit)
    return values_in


def gather_down(values_in, high_bit, leaf_pos):
    for bit in range(0, high_bit):
        partner = from_partner(values_in, "leaf", bit)
        values_in = pair_order(values_in, partner, leaf_pos, bit)
    return values_in


def sum_range(partial_value, high_bit):
    for bit in range(0, high_bit):
        partial_value = partial_value + from_partner(partial_value, "leaf", bit)
    return partial_value


def local(
    points,
    coefs,
    targets,
    ridge,
    tile_mask,
    cluster_perm,
    leaf_map,
    leaf_inverse,
    leaf_basis,
    node_inverse,
    node_transfer,
):
    col_count = lax.axis_size("col")
    col_pos = lax.axis_index("col")
    leaf_count = lax.axis_size("leaf")
    leaf_pos = lax.axis_index("leaf")
    gathered = (
        lax.all_gather(points, "col", axis=0, tiled=True),
        lax.all_gather(coefs, "col", axis=0, tiled=True),
        lax.all_gather(targets, "col", axis=0, tiled=True),
    )
    cluster_order = cluster_perm[0]
    ordered_x = gathered[0][cluster_order]
    ordered_a = gathered[1][cluster_order]
    ordered_y = gathered[2][cluster_order]
    leaf_size, features = ordered_x.shape
    target_width = ordered_a.shape[1]
    share_rows = leaf_size // col_count
    col_width = target_width // col_count
    band_reach = tile_mask.shape[1] // 2
    own_rows = jnp.concatenate(
        [
            lax.dynamic_slice_in_dim(ordered_x, col_pos * share_rows, share_rows, 0),
            lax.dynamic_slice_in_dim(ordered_a, col_pos * share_rows, share_rows, 0),
        ],
        axis=1,
    )
    fetched = [own_rows for band_slot in range(2 * band_reach + 1)]
    for offset in range(-band_reach, band_reach + 1):
        if offset != 0:
            fetched[offset + band_reach] = shifted(own_rows, "leaf", -offset)
    row_squares = jnp.sum(ordered_x * ordered_x, axis=1)

    def tile_term(packed):
        column_points = packed[:, :features]
        kernel = kernel_tile(
            ordered_x, row_squares, column_points, jnp.sum(column_points * column_points, axis=1)
        )
        return jnp.dot(kernel, packed[:, features:], precision=highest)

    def no_term(packed):
        return jnp.zeros((leaf_size, target_width), jnp.float32)

    tile_total = jnp.zeros((leaf_size, target_width), jnp.float32)
    for band_slot in range(2 * band_reach + 1):
        tile_total = tile_total + lax.cond(
            tile_mask[0, band_slot] > 0, tile_term, no_term, fetched[band_slot]
        )
    summed = lax.psum_scatter(tile_total, "col", scatter_dimension=1, tiled=True)
    a_cols = lax.dynamic_slice_in_dim(ordered_a, col_pos * col_width, col_width, 1)
    y_cols = lax.dynamic_slice_in_dim(ordered_y, col_pos * col_width, col_width, 1)
    residual_c = y_cols - ridge[0] * a_cols - summed
    leaf_solve = leaf_inverse[0]
    basis = leaf_basis[0]
    rank_size = basis.shape[1]
    solved = jnp.dot(leaf_solve, residual_c, precision=highest)
    reduced = jnp.einsum("lr,lc->rc", basis, solved, precision=highest)
    group_base = leaf_pos // 4 * 4
    tree_slots = lax.dynamic_slice_in_dim(leaf_map, group_base, 4, 0) - group_base
    levels = tree_levels(leaf_count, rank_size)
    current = reduced
    stored = []
    child_log = 0
    for height, children, covered, offset, slice_count in levels:
        span_log = covered.bit_length() - 1
        node_rows = children * rank_size
        stacked = gather_up(current, child_log, span_log, leaf_pos)
        if height == 1:
            stacked = stacked.reshape(children, rank_size, col_width)[tree_slots].reshape(
                node_rows, col_width
            )
        node_inv = node_inverse[0, offset : offset + slice_count, :node_rows]
        transfer_rows = node_transfer[0, offset : offset + slice_count]
        weights = jnp.dot(node_inv, stacked, precision=highest)
        stored.append((weights, node_inv, transfer_rows))
        if height < len(levels):
            partial_value = jnp.einsum("ar,ac->rc", transfer_rows, weights, precision=highest)
            current = sum_range(partial_value, span_log)
        child_log = span_log
    values = stored[-1][0]
    for position in range(len(levels) - 1, 0, -1):
        child_covered = levels[position - 1][2]
        child_span_log = child_covered.bit_length() - 1
        child_weights, child_inv, child_transfer = stored[position - 1]
        parent_rows = gather_down(values, child_span_log, leaf_pos)
        lifted_rows = jnp.dot(child_transfer, parent_rows, precision=highest)
        lifted = gather_down(lifted_rows, child_span_log, leaf_pos)
        values = child_weights - jnp.dot(child_inv, lifted, precision=highest)
    all_pieces = gather_down(values, 2, leaf_pos)
    local_index = leaf_pos - group_base
    four = jnp.arange(4, dtype=jnp.int32)
    own_slot = jnp.sum(four * (tree_slots == local_index).astype(jnp.int32))
    incoming = lax.dynamic_slice_in_dim(all_pieces, own_slot * rank_size, rank_size, 0)
    lifted = jnp.dot(basis, incoming, precision=highest)
    correction = jnp.dot(leaf_solve, lifted, precision=highest)
    fresh = a_cols + (solved - correction)
    inverse = (
        jnp.zeros((leaf_size,), jnp.int32)
        .at[cluster_order]
        .set(jnp.arange(leaf_size, dtype=jnp.int32))
    )
    residual_back = residual_c[inverse]
    fresh_back = fresh[inverse]
    full_residual, full_fresh = (
        lax.all_gather(residual_back, "col", axis=1, tiled=True),
        lax.all_gather(fresh_back, "col", axis=1, tiled=True),
    )
    residual_rows = lax.dynamic_slice_in_dim(full_residual, col_pos * share_rows, share_rows, 0)
    fresh_rows = lax.dynamic_slice_in_dim(full_fresh, col_pos * share_rows, share_rows, 0)
    return (residual_rows, fresh_rows)


def solution(mesh):
    return jax.shard_map(
        local,
        mesh=mesh,
        in_specs=(
            P(("leaf", "col"), None),
            P(("leaf", "col"), None),
            P(("leaf", "col"), None),
            P(),
            P("leaf", None),
            P("leaf", None),
            P(),
            P("leaf", None, None),
            P("leaf", None, None),
            P("leaf", None, None),
            P("leaf", None, None),
        ),
        out_specs=(P(("leaf", "col"), None), P(("leaf", "col"), None)),
        check_vma=False,
    )
```

profile of v0, /device:TPU:0, one launch (start us, length us, event | category | flops | bytes accessed | tf_op | source)
XLA Modules:
  0.0 259.8 jit_solution(6797572461202957209)
XLA Ops:
  8.7 8.9 %all_gather.17 = f32[1024,128]{1,0:T(8,128)S(1)} all-gather(f32[256,128]{1,0:T(8,128)} %param.21), channel_id=1, replica_groups=mesh['leaf'=8,'col'=4] {'col'}, dimensions={0}, use_global_device_ids=true | all-gather | bytes 655360 | tf_op jit(solution)/shard_map/all_gather | solution.py:92
  18.3 2.8 %gather_fusion.2 = f32[1024,128]{1,0:T(8,128)S(1)} fusion(f32[1024,128]{1,0:T(8,128)S(1)} %all_gather.17, s32[1024]{0:T(1024)S(1)} %broadcast_clamp_fusion), kind=kCustom, calls=%fused_computation.2 | custom fusion | bytes 1052672 | tf_op jit(solution)/shard_map/gather | solution.py:97
  21.1 13.8 %all-gather.9.cloned.1.call-done = f32[1024,512]{1,0:T(8,128)} async-done(((f32[256,512]{1,0:T(8,128)}), f32[1024,512]{1,0:T(8,128)}) %all-gather.9.cloned.1.call-update) | async-done | bytes 2097168 | tf_op jit(solution)/shard_map/all_gather | solution.py:93
  34.9 6.9 %gather_fusion.1 = f32[1024,512]{1,0:T(8,128)} fusion(f32[1024,512]{1,0:T(8,128)} %all-gather.9.cloned.1.call-done, s32[1024]{0:T(1024)S(1)} %broadcast_clamp_fusion), kind=kCustom, calls=%fused_computation.1 | custom fusion | bytes 4198400 | tf_op jit(solution)/shard_map/gather | solution.py:98
  43.8 4.2 %collective-permute-start = (f32[256,640]{1,0:T(8,128)}, f32[256,640]{1,0:T(8,128)}, u32[]{:S(2)}, u32[]{:S(2)}) collective-permute-start(f32[256,640]{1,0:T(8,128)} %pad_maximum_fusion), channel_id=1, source_target_pairs={{0,8},{4,12},{8,16},{12,20},{16,24},{20,28},{1,9},{5,13},{9,17},{1... | collective-permute-start | bytes 1966088 | tf_op jit(solution)/shard_map/ppermute | solution.py:22
  48.1 4.3 %collective-permute-start.1 = (f32[256,640]{1,0:T(8,128)}, f32[256,640]{1,0:T(8,128)}, u32[]{:S(2)}, u32[]{:S(2)}) collective-permute-start(f32[256,640]{1,0:T(8,128)} %pad_maximum_fusion), channel_id=1, source_target_pairs={{0,4},{4,8},{8,12},{12,16},{16,20},{20,24},{24,28},{1,5},{5,9},{9,... | collective-permute-start | bytes 1966088 | tf_op jit(solution)/shard_map/ppermute | solution.py:22
  59.0 3.1 %conditional.7 = (f32[1024,512]{0,1:T(8,128)S(1)}) conditional(s32[]{:T(128)} %bitcast.5, () %tuple.42, (f32[1024]{0:T(1024)S(1)}, f32[256,128]{1,0:T(8,128)S(1)}, f32[1024,128]{1,0:T(8,128)S(1)}, f32[256,512]{1,0:T(8,128)S(1)}) %tuple.43), branch_computations={%region_7.0_spmd, %region_8.0_spmd} | conditional | flops 2014379776 | bytes 5511176 | solution.py:130
  63.7 16.2 %collective-permute-done.1 = f32[256,640]{1,0:T(8,128)} collective-permute-done((f32[256,640]{1,0:T(8,128)}, f32[256,640]{1,0:T(8,128)}, u32[]{:S(2)}, u32[]{:S(2)}) %collective-permute-start.1) | collective-permute-done | bytes 655392 | tf_op jit(solution)/shard_map/ppermute | solution.py:22
  81.5 3.1 %conditional.8 = (f32[1024,512]{0,1:T(8,128)S(1)}) conditional(s32[]{:T(128)} %bitcast.6, () %tuple.44, (f32[1024]{0:T(1024)S(1)}, f32[256,640]{1,0:T(8,128)S(1)}, f32[1024,128]{1,0:T(8,128)S(1)}) %tuple.45), branch_computations={%region_10.0_spmd, %region_11.0_spmd} | conditional | flops 2014379776 | bytes 5511176 | solution.py:130
  86.0 4.4 %conditional.9 = (f32[1024,512]{0,1:T(8,128)}) conditional(s32[]{:T(128)} %bitcast.7, () %tuple.46, (f32[1024]{0:T(1024)S(1)}, f32[256,640]{1,0:T(8,128)S(1)}, f32[1024,128]{1,0:T(8,128)S(1)}) %tuple.47), branch_computations={%region_13.0_spmd, %region_14.0_spmd} | conditional | flops 2014379776 | bytes 5511176 | solution.py:130
  87.1 3.2 %fusion.24 = f32[1024,512]{0,1:T(8,128)} fusion(f32[1024,256]{1,0:T(8,128)S(1)} %fusion.23, f32[256,640]{1,0:T(8,128)S(1)} %get-tuple-element.61), kind=kOutput, calls=%fused_computation.40 | convolution fusion | flops 1610612736 | bytes 3670016 | tf_op jit(solution)/shard_map/cond | solution.py:130
  90.3 6.8 %add_add_fusion = f32[1024,512]{0,1:T(8,128)} fusion(f32[1024,512]{0,1:T(8,128)} %get-tuple-element.69, f32[1024,512]{0,1:T(8,128)} %copy-done.4, f32[1024,512]{0,1:T(8,128)} %copy-done.1, f32[1024,512]{0,1:T(8,128)} %copy-done.2, f32[1024,512]{0,1:T(8,128)} %copy-done.3), kind=kLoop, calls=%fused_computation.48 | loop fusion | flops 2097152 | bytes 12582912 | tf_op jit(solution)/shard_map/add | solution.py:130
  98.1 5.6 %gather_fusion = f32[1024,512]{1,0:T(8,128)S(1)} fusion(f32[1024,512]{1,0:T(8,128)} %all-gather.7.cloned.1.call-done, s32[1024]{0:T(1024)S(1)} %broadcast_clamp_fusion), kind=kCustom, calls=%fused_computation | custom fusion | bytes 4198400 | tf_op jit(solution)/shard_map/gather | solution.py:99
  107.1 26.5 %reduce-scatter.2.cloned.1.call-done = f32[1024,128]{0,1:T(8,128)} async-done(((f32[1024,512]{0,1:T(8,128)}), f32[1024,128]{0,1:T(8,128)}) %reduce-scatter.2.cloned.1.call-update) | async-done | bytes 524304 | tf_op jit(solution)/shard_map/reduce_scatter | solution.py:133
  134.8 6.5 %fusion.29 = f32[128,1024]{1,0:T(8,128)S(1)} fusion(f32[1024,128]{0,1:T(8,128)S(1)} %subtract_subtract_fusion, f32[1,1024,1024]{2,1,0:T(8,128)} %param.28), kind=kOutput, calls=%fused_computation.46 | convolution fusion | flops 1610612736 | bytes 5242880 | tf_op jit(solution)/shard_map/dot_general | solution.py:140
  143.6 3.8 %collective-permute-done.4 = f32[256,128]{0,1:T(8,128)S(1)} collective-permute-done((f32[256,128]{0,1:T(8,128)S(1)}, f32[256,128]{0,1:T(8,128)S(1)}, u32[]{:S(2)}, u32[]{:S(2)}) %collective-permute-start.4) | collective-permute-done | bytes 131104 | tf_op jit(solution)/shard_map/ppermute | solution.py:16
  149.7 4.9 %collective-permute-done.5 = f32[512,128]{0,1:T(8,128)S(1)} collective-permute-done((f32[512,128]{0,1:T(8,128)S(1)}, f32[512,128]{0,1:T(8,128)S(1)}, u32[]{:S(2)}, u32[]{:S(2)}) %collective-permute-start.5) | collective-permute-done | bytes 262176 | tf_op jit(solution)/shard_map/ppermute | solution.py:16
  157.3 2.2 fusion.42
  162.4 3.5 %collective-permute-done.6 = f32[256,128]{0,1:T(8,128)S(1)} collective-permute-done((f32[256,128]{0,1:T(8,128)S(1)}, f32[256,128]{0,1:T(8,128)S(1)}, u32[]{:S(2)}, u32[]{:S(2)}) %collective-permute-start.6) | collective-permute-done | bytes 131104 | tf_op jit(solution)/shard_map/ppermute | solution.py:16
  167.5 4.8 %collective-permute-done.7 = f32[256,128]{0,1:T(8,128)S(1)} collective-permute-done((f32[256,128]{0,1:T(8,128)S(1)}, f32[256,128]{0,1:T(8,128)S(1)}, u32[]{:S(2)}, u32[]{:S(2)}) %collective-permute-start.7) | collective-permute-done | bytes 131104 | tf_op jit(solution)/shard_map/ppermute | solution.py:16
  172.3 2.3 collective-permute-start.8
  174.7 5.0 %collective-permute-done.8 = f32[256,128]{0,1:T(8,128)S(1)} collective-permute-done((f32[256,128]{0,1:T(8,128)S(1)}, f32[256,128]{0,1:T(8,128)S(1)}, u32[]{:S(2)}, u32[]{:S(2)}) %collective-permute-start.8) | collective-permute-done | bytes 131104 | tf_op jit(solution)/shard_map/ppermute | solution.py:16
  182.5 4.3 %scatter_custom_fusion = s32[1024]{0:T(1024)S(1)} fusion(s32[1024]{0:T(1024)S(1)} %bitcast.76, s32[1024]{0:T(1024)S(1)} %iota.6, s32[]{:T(128)} %constant.135.clone.1), kind=kCustom, calls=%fused_computation.116 | custom fusion | bytes 4100 | tf_op jit(solution)/shard_map/scatter | solution.py:184
  187.1 4.0 %gather_fusion.3 = f32[1024,128]{1,0:T(8,128)} fusion(f32[1024,128]{1,0:T(8,128)S(1)} %copy.29, s32[1024]{0:T(1024)S(1)} %fusion.66), kind=kCustom, calls=%fused_computation.3 | custom fusion | bytes 1052672 | tf_op jit(solution)/shard_map/gather | solution.py:186
  192.6 4.4 %collective-permute-done.11 = f32[256,128]{0,1:T(8,128)S(1)} collective-permute-done((f32[256,128]{0,1:T(8,128)S(1)}, f32[256,128]{0,1:T(8,128)S(1)}, u32[]{:S(2)}, u32[]{:S(2)}) %collective-permute-start.11) | collective-permute-done | bytes 131104 | tf_op jit(solution)/shard_map/ppermute | solution.py:16
  199.1 6.2 %collective-permute-done.12 = f32[512,128]{0,1:T(8,128)S(1)} collective-permute-done((f32[512,128]{0,1:T(8,128)S(1)}, f32[512,128]{0,1:T(8,128)S(1)}, u32[]{:S(2)}, u32[]{:S(2)}) %collective-permute-start.12) | collective-permute-done | bytes 262176 | tf_op jit(solution)/shard_map/ppermute | solution.py:16
  207.1 4.5 %collective-permute-done.13 = f32[256,128]{0,1:T(8,128)S(1)} collective-permute-done((f32[256,128]{0,1:T(8,128)S(1)}, f32[256,128]{0,1:T(8,128)S(1)}, u32[]{:S(2)}, u32[]{:S(2)}) %collective-permute-start.13) | collective-permute-done | bytes 131104 | tf_op jit(solution)/shard_map/ppermute | solution.py:16
  211.7 2.6 collective-permute-start.14
  214.9 3.7 %collective-permute-done.14 = f32[512,128]{0,1:T(8,128)S(1)} collective-permute-done((f32[512,128]{0,1:T(8,128)S(1)}, f32[512,128]{0,1:T(8,128)S(1)}, u32[]{:S(2)}, u32[]{:S(2)}) %collective-permute-start.14) | collective-permute-done | bytes 262176 | tf_op jit(solution)/shard_map/ppermute | solution.py:16
  219.8 6.6 %fusion.37 = f32[1024,128]{0,1:T(8,128)S(1)} fusion(f32[1024,128]{0,1:T(8,128)S(1)} %copy.44, f32[128,1024]{1,0:T(8,128)S(1)} %fusion.29, f32[128,1024]{1,0:T(8,128)S(1)} %fusion.44, f32[1,1024,1024]{2,1,0:T(8,128)} %param.28), kind=kOutput, calls=%fused_computation.51 | convolution fusion | flops 1610874880 | bytes 6291456 | tf_op jit(solution)/shard_map/dot_general | solution.py:179
  226.6 4.0 %gather_fusion.5 = f32[1024,128]{1,0:T(8,128)} fusion(f32[1024,128]{1,0:T(8,128)S(1)} %copy.31, s32[1024]{0:T(1024)S(1)} %fusion.66), kind=kCustom, calls=%fused_computation.5 | custom fusion | bytes 1052672 | tf_op jit(solution)/shard_map/gather | solution.py:187
  232.5 18.9 %all-gather.13.cloned.1.call-done = f32[1024,512]{1,0:T(8,128)} async-done(((f32[1024,128]{1,0:T(8,128)}), f32[1024,512]{1,0:T(8,128)}) %all-gather.13.cloned.1.call-update) | async-done | bytes 2097168 | tf_op jit(solution)/shard_map/all_gather | solution.py:190
  (102 shorter events, 50.1 us)
Async XLA Ops:
  7.2 134.2 %copy-start = (f32[1,1024,256]{2,1,0:T(8,128)S(1)}, f32[1,1024,256]{2,1,0:T(8,128)}, u32[]{:S(2)}) copy-start(f32[1,1024,256]{2,1,0:T(8,128)} %param.29) | copy-start | bytes 3145732
  7.2 27.7 %all-gather.9.cloned.1.call-start = ((), (), s32[]{:S(2)}) async-start(), calls=%async_computation.2 | async-start | bytes 2621440 | tf_op jit(solution)/shard_map/all_gather | solution.py:93
  7.9 90.2 %all-gather.7.cloned.1.call-start = ((), (), s32[]{:S(2)}) async-start(), calls=%async_computation.1 | async-start | bytes 2621440 | tf_op jit(solution)/shard_map/all_gather | solution.py:94
  8.7 125.0 %reduce-scatter.2.cloned.1.call-start = ((), (), s32[]{:S(2)}) async-start(), calls=%async_computation.3 | async-start | bytes 2621440 | tf_op jit(solution)/shard_map/reduce_scatter | solution.py:133
  41.8 13.2 %copy-start.7 = (s32[1,5]{1,0:T(1,128)S(1)}, s32[1,5]{1,0:T(1,128)}, u32[]{:S(2)}) copy-start(s32[1,5]{1,0:T(1,128)} %param.25) | copy-start | bytes 64
  43.8 18.2 %collective-permute-start = (f32[256,640]{1,0:T(8,128)}, f32[256,640]{1,0:T(8,128)}, u32[]{:S(2)}, u32[]{:S(2)}) collective-permute-start(f32[256,640]{1,0:T(8,128)} %pad_maximum_fusion), channel_id=1, source_target_pairs={{0,8},{4,12},{8,16},{12,20},{16,24},{20,28},{1,9},{5,13},{9,17},{1... | collective-permute-start | bytes 1966088 | tf_op jit(solution)/shard_map/ppermute | solution.py:22
  48.1 31.8 %collective-permute-start.1 = (f32[256,640]{1,0:T(8,128)}, f32[256,640]{1,0:T(8,128)}, u32[]{:S(2)}, u32[]{:S(2)}) collective-permute-start(f32[256,640]{1,0:T(8,128)} %pad_maximum_fusion), channel_id=1, source_target_pairs={{0,4},{4,8},{8,12},{12,16},{16,20},{20,24},{24,28},{1,5},{5,9},{9,... | collective-permute-start | bytes 1966088 | tf_op jit(solution)/shard_map/ppermute | solution.py:22
  52.4 27.8 %collective-permute-start.2 = (f32[256,640]{1,0:T(8,128)}, f32[256,640]{1,0:T(8,128)S(1)}, u32[]{:S(2)}, u32[]{:S(2)}) collective-permute-start(f32[256,640]{1,0:T(8,128)} %pad_maximum_fusion), channel_id=1, source_target_pairs={{4,0},{8,4},{12,8},{16,12},{20,16},{24,20},{28,24},{5,1},{9,5},{13... | collective-permute-start | bytes 1966088 | tf_op jit(solution)/shard_map/ppermute | solution.py:22
  53.6 31.0 %collective-permute-start.3 = (f32[256,640]{1,0:T(8,128)}, f32[256,640]{1,0:T(8,128)S(1)}, u32[]{:S(2)}, u32[]{:S(2)}) collective-permute-start(f32[256,640]{1,0:T(8,128)} %pad_maximum_fusion), channel_id=1, source_target_pairs={{8,0},{12,4},{16,8},{20,12},{24,16},{28,20},{9,1},{13,5},{17,9},{2... | collective-permute-start | bytes 1966088 | tf_op jit(solution)/shard_map/ppermute | solution.py:22
  62.0 1.4 copy-start.1
  63.7 16.2 %copy-start.2 = (f32[1024,512]{0,1:T(8,128)}, f32[1024,512]{0,1:T(8,128)S(1)}, u32[]{:S(2)}) copy-start(f32[1024,512]{0,1:T(8,128)S(1)} %get-tuple-element.65) | copy-start | bytes 6291460
  80.2 1.4 copy-start.3
  84.6 1.4 copy-start.4
  97.1 133.5 %all-gather.11.cloned.1.call-start = ((), (), s32[]{:S(2)}) async-start(), calls=%async_computation.4 | async-start | bytes 2621440 | tf_op jit(solution)/shard_map/all_gather | solution.py:189
  141.4 7.6 %copy-start.8 = (s32[8]{0:T(128)S(1)}, s32[8]{0:T(128)}, u32[]{:S(2)}) copy-start(s32[8]{0:T(128)} %param.27) | copy-start | bytes 100
  142.0 5.3 %collective-permute-start.4 = (f32[256,128]{0,1:T(8,128)S(1)}, f32[256,128]{0,1:T(8,128)S(1)}, u32[]{:S(2)}, u32[]{:S(2)}) collective-permute-start(f32[256,128]{0,1:T(8,128)S(1)} %convolution_bitcast_fusion.2), channel_id=1, source_target_pairs={{0,4},{4,0},{8,12},{12,8},{16,20},{20,16},{24,28},{28,24},{1,5},{5... | collective-permute-start | bytes 393224 | tf_op jit(solution)/shard_map/ppermute | solution.py:16
  147.4 7.2 %collective-permute-start.5 = (f32[512,128]{0,1:T(8,128)S(1)}, f32[512,128]{0,1:T(8,128)S(1)}, u32[]{:S(2)}, u32[]{:S(2)}) collective-permute-start(f32[512,128]{0,1:T(8,128)S(1)} %pad_maximum_fusion.2), channel_id=1, source_target_pairs={{0,8},{8,0},{4,12},{12,4},{16,24},{24,16},{20,28},{28,20},{1,9},{9... | collective-permute-start | bytes 786440 | tf_op jit(solution)/shard_map/ppermute | solution.py:16
  160.8 5.0 %collective-permute-start.6 = (f32[256,128]{0,1:T(8,128)S(1)}, f32[256,128]{0,1:T(8,128)S(1)}, u32[]{:S(2)}, u32[]{:S(2)}) collective-permute-start(f32[256,128]{0,1:T(8,128)S(1)} %convolution_bitcast_fusion.1), channel_id=1, source_target_pairs={{0,4},{4,0},{8,12},{12,8},{16,20},{20,16},{24,28},{28,24},{1,5},{5... | collective-permute-start | bytes 393224 | tf_op jit(solution)/shard_map/ppermute | solution.py:16
  165.8 6.4 %collective-permute-start.7 = (f32[256,128]{0,1:T(8,128)S(1)}, f32[256,128]{0,1:T(8,128)S(1)}, u32[]{:S(2)}, u32[]{:S(2)}) collective-permute-start(f32[256,128]{0,1:T(8,128)S(1)} %add.156), channel_id=1, source_target_pairs={{0,8},{8,0},{4,12},{12,4},{16,24},{24,16},{20,28},{28,20},{1,9},{9... | collective-permute-start | bytes 393224 | tf_op jit(solution)/shard_map/ppermute | solution.py:16
  172.3 7.3 %collective-permute-start.8 = (f32[256,128]{0,1:T(8,128)S(1)}, f32[256,128]{0,1:T(8,128)S(1)}, u32[]{:S(2)}, u32[]{:S(2)}) collective-permute-start(f32[256,128]{0,1:T(8,128)S(1)} %add.157), channel_id=1, source_target_pairs={{0,16},{16,0},{4,20},{20,4},{8,24},{24,8},{12,28},{28,12},{1,17},{... | collective-permute-start | bytes 393224 | tf_op jit(solution)/shard_map/ppermute | solution.py:16
  181.0 5.8 %collective-permute-start.9 = (f32[64,128]{1,0:T(8,128)S(1)}, f32[64,128]{1,0:T(8,128)S(1)}, u32[]{:S(2)}, u32[]{:S(2)}) collective-permute-start(f32[64,128]{1,0:T(8,128)S(1)} %convolution_bitcast_fusion.3), channel_id=1, source_target_pairs={{0,4},{4,0},{8,12},{12,8},{16,20},{20,16},{24,28},{28,24},{1,5},{5... | collective-permute-start | bytes 98312 | tf_op jit(solution)/shard_map/ppermute | solution.py:16
  186.8 4.7 %collective-permute-start.10 = (f32[128,128]{1,0:T(8,128)S(1)}, f32[128,128]{1,0:T(8,128)S(1)}, u32[]{:S(2)}, u32[]{:S(2)}) collective-permute-start(f32[128,128]{1,0:T(8,128)S(1)} %pad_maximum_fusion.5), channel_id=1, source_target_pairs={{0,8},{8,0},{4,12},{12,4},{16,24},{24,16},{20,28},{28,20},{1,9},{9... | collective-permute-start | bytes 196616 | tf_op jit(solution)/shard_map/ppermute | solution.py:16
  187.1 4.4 %copy-start.6 = (f32[1,320,256]{2,1,0:T(8,128)S(1)}, f32[1,320,256]{2,1,0:T(8,128)}, u32[]{:S(2)}) copy-start(f32[1,320,256]{2,1,0:T(8,128)} %param.31) | copy-start | bytes 983044
  191.2 60.2 %all-gather.13.cloned.1.call-start = ((), (), s32[]{:S(2)}) async-start(), calls=%async_computation.5 | async-start | bytes 2621440 | tf_op jit(solution)/shard_map/all_gather | solution.py:190
  191.5 13.9 %copy-start.5 = (f32[1,320,1024]{2,1,0:T(8,128)S(1)}, f32[1,320,1024]{2,1,0:T(8,128)}, u32[]{:S(2)}) copy-start(f32[1,320,1024]{2,1,0:T(8,128)} %param.30) | copy-start | bytes 3932164
  192.0 5.0 %collective-permute-start.11 = (f32[256,128]{0,1:T(8,128)S(1)}, f32[256,128]{0,1:T(8,128)S(1)}, u32[]{:S(2)}, u32[]{:S(2)}) collective-permute-start(f32[256,128]{0,1:T(8,128)S(1)} %convolution_bitcast_fusion), channel_id=1, source_target_pairs={{0,4},{4,0},{8,12},{12,8},{16,20},{20,16},{24,28},{28,24},{1,5},{5... | collective-permute-start | bytes 393224 | tf_op jit(solution)/shard_map/ppermute | solution.py:16
  197.1 8.3 %collective-permute-start.12 = (f32[512,128]{0,1:T(8,128)S(1)}, f32[512,128]{0,1:T(8,128)S(1)}, u32[]{:S(2)}, u32[]{:S(2)}) collective-permute-start(f32[512,128]{0,1:T(8,128)S(1)} %pad_maximum_fusion.3), channel_id=1, source_target_pairs={{0,8},{8,0},{4,12},{12,4},{16,24},{24,16},{20,28},{28,20},{1,9},{9... | collective-permute-start | bytes 786440 | tf_op jit(solution)/shard_map/ppermute | solution.py:16
  206.6 5.0 %collective-permute-start.13 = (f32[256,128]{0,1:T(8,128)S(1)}, f32[256,128]{0,1:T(8,128)S(1)}, u32[]{:S(2)}, u32[]{:S(2)}) collective-permute-start(f32[256,128]{0,1:T(8,128)S(1)} %fusion.40), channel_id=1, source_target_pairs={{0,4},{4,0},{8,12},{12,8},{16,20},{20,16},{24,28},{28,24},{1,5},{5... | collective-permute-start | bytes 393224 | tf_op jit(solution)/shard_map/ppermute | solution.py:16
  211.7 6.9 %collective-permute-start.14 = (f32[512,128]{0,1:T(8,128)S(1)}, f32[512,128]{0,1:T(8,128)S(1)}, u32[]{:S(2)}, u32[]{:S(2)}) collective-permute-start(f32[512,128]{0,1:T(8,128)S(1)} %pad_maximum_fusion.4), channel_id=1, source_target_pairs={{0,8},{8,0},{4,12},{12,4},{16,24},{24,16},{20,28},{28,20},{1,9},{9... | collective-permute-start | bytes 786440 | tf_op jit(solution)/shard_map/ppermute | solution.py:16
Sparse Core Ops, SparseCore 0:
  9.6 25.2 all-gather.8
  36.5 22.5 all-gather.6
  97.3 36.3 reduce-scatter.1
  191.3 21.7 all-gather.10
  230.7 20.6 all-gather.12
where the time goes:
time: 261 us; the launch traced here: 260 us
  waiting for transfers between devices  118 us (45%)
  local copies, waits for them, and re-layouts  44.2 us (17%)
  matrix products  31.4 us (12%)
  starting transfers between devices  27.7 us (11%)
  between operations  18.7 us (7%)
  other arithmetic  11.2 us (4%)
  blocking collectives  8.86 us (3%)
    ppermute x11, waiting for transfers between devices, from_partner(): return lax.ppermute(block, axis, route)  40.8 us
    reduce_scatter x1, waiting for transfers between devices, local(): lax.psum_scatter(tile_total, 'col', scatter_dimension=1, tiled=True)  26.5 us
    all_gather x1, waiting for transfers between devices, local(): lax.all_gather(fresh_back, 'col', axis=1, tiled=True)  18.9 us
    ppermute x4, waiting for transfers between devices, shifted(): lax.ppermute(value, axis, [(source, source + steps) for source in range(i...  16.2 us
    ppermute x11, starting transfers between devices, from_partner(): return lax.ppermute(block, axis, route)  16 us
    all_gather x1, waiting for transfers between devices, local(): lax.all_gather(coefs, 'col', axis=0, tiled=True)  13.8 us
    ppermute x4, starting transfers between devices, shifted(): lax.ppermute(value, axis, [(source, source + steps) for source in range(i...  11.1 us
    all_gather x1, blocking collectives, local(): lax.all_gather(points, 'col', axis=0, tiled=True)  8.86 us
  transfers between devices with their start and end apart: 20, of which 13 were waited for; matrix products, arithmetic and copies ran while one was open for 25% of the time, Pallas kernels for 0%

commit v1 on v0

v1 whole, which is shorter than its diff:
```python
import jax
import jax.numpy as jnp
from jax import lax
from jax.sharding import PartitionSpec as P

high = lax.Precision.HIGH


def swap_route(count, mask):
    return [(place, place ^ mask) for place in range(count)]


def partner_of(block, axis, mask):
    return lax.ppermute(block, axis, swap_route(lax.axis_size(axis), mask))


def shifted(value, axis, steps):
    count = lax.axis_size(axis)
    initial, last = (max(0, -steps), min(count, count - steps))
    return lax.ppermute(value, axis, [(source, source + steps) for source in range(initial, last)])


def exchange_raw(block, axis, low, fan):
    return [block] + [partner_of(block, axis, m << low) for m in range(1, fan)]


def in_order(pieces, digit):
    pieces = list(pieces)
    bit = 0
    while 1 << bit < len(pieces):
        odd = (digit >> bit) % 2 == 1
        pieces = [jnp.where(odd, pieces[m ^ (1 << bit)], pieces[m]) for m in range(len(pieces))]
        bit += 1
    return pieces


def exchange(block, axis, pos, low, fan):
    return in_order(exchange_raw(block, axis, low, fan), (pos >> low) % fan)


def tree_levels(remaining, rank_size):
    levels = []
    covered = 1
    offset = 0
    while remaining > 1:
        children = 4 if remaining % 4 == 0 else remaining
        low = covered.bit_length() - 1
        covered = covered * children
        remaining = remaining // children
        slice_count = children * rank_size // covered
        levels.append((children, low, offset, slice_count))
        offset = offset + slice_count
    return levels


def mm(a, b):
    return jnp.dot(a, b, precision=high)


def mm_t(a, b):
    return jnp.einsum("ka,kc->ac", a, b, precision=high)


def to_rows(block, col_pos, col_count):
    share = block.shape[0] // col_count
    width = block.shape[1]
    out = jnp.zeros((share, width * col_count), block.dtype)
    for m in range(col_count):
        target = col_pos ^ m
        piece = lax.dynamic_slice_in_dim(block, target * share, share, 0)
        if m:
            piece = partner_of(piece, "col", m)
        out = lax.dynamic_update_slice(out, piece, (0, target * width))
    return out


def local(
    points,
    coefs,
    targets,
    ridge,
    tile_mask,
    cluster_perm,
    leaf_map,
    leaf_inverse,
    leaf_basis,
    node_inverse,
    node_transfer,
):
    col_count = lax.axis_size("col")
    col_pos = lax.axis_index("col")
    leaf_count = lax.axis_size("leaf")
    leaf_pos = lax.axis_index("leaf")
    share_rows, features = points.shape
    leaf_size = share_rows * col_count
    target_width = coefs.shape[1]
    col_width = target_width // col_count
    band_reach = tile_mask.shape[1] // 2
    scale = -2.0 / features

    packed = jnp.concatenate([points, coefs], axis=1)
    fetched = {0: packed}
    for offset in range(-band_reach, band_reach + 1):
        if offset != 0:
            fetched[offset] = shifted(packed, "leaf", -offset)
    rows_x = lax.all_gather(points, "col", axis=0, tiled=True)
    row_squares = jnp.sum(rows_x * rows_x, axis=1)

    def kernel_of(offset):
        column_points = fetched[offset][:, :features]
        squares = jnp.sum(column_points * column_points, axis=1)
        inner = jnp.einsum("pf,qf->pq", rows_x, column_points, precision=high)
        values = jnp.exp((row_squares[:, None] + squares[None, :] - 2.0 * inner) * scale)
        return jnp.where(tile_mask[0, offset + band_reach] > 0, values, 0.0)

    basis = leaf_basis[0]
    solve = leaf_inverse[0]
    rank_size = basis.shape[1]
    order = cluster_perm[0]
    spread = (order[:, None] == jnp.arange(leaf_size, dtype=jnp.int32)[None, :]).astype(jnp.float32)
    down_map = mm_t(spread, mm(solve, basis))
    up_map = mm(mm_t(basis, solve), spread)

    levels = tree_levels(leaf_count, rank_size)
    share_rank = rank_size // col_count
    shared = []
    for number, (children, low, offset, slice_count) in enumerate(levels):
        node_rows = children * rank_size
        node_inv = node_inverse[0, offset : offset + slice_count, :node_rows]
        if number > 0:
            part = slice_count // col_count
            mine = lax.dynamic_slice_in_dim(node_inv, col_pos * part, part, 0)[None]
            for below in range(number):
                fan, below_low = levels[below][:2]
                mine = jnp.concatenate(exchange(mine, "leaf", leaf_pos, below_low, fan), axis=0)
            every = lax.all_gather(mine, "col", axis=1, tiled=True)
            own_inv = every.reshape(rank_size, node_rows)
        else:
            own_inv = node_inv
        lift = None
        merge = None
        if number < len(levels) - 1:
            transfer = lax.dynamic_slice(
                node_transfer[0], (offset, col_pos * share_rank), (slice_count, share_rank)
            ).T
            part_merge = mm(transfer, node_inv)
            whole = transfer
            for fan, digit_low in [level[:2] for level in levels[: number + 1]]:
                whole = jnp.concatenate(exchange(whole, "leaf", leaf_pos, digit_low, fan), axis=1)
                for bit in range(fan.bit_length() - 1):
                    part_merge = part_merge + partner_of(part_merge, "leaf", 1 << (digit_low + bit))
            part_lift = jnp.einsum("ra,ba->rb", whole, own_inv, precision=high)
            both = lax.all_gather(
                jnp.concatenate([part_merge, part_lift], axis=1), "col", axis=0, tiled=True
            )
            merge = both[:, :node_rows]
            lift = both[:, node_rows:]
        shared.append((own_inv, merge, lift))

    base = targets - ridge[0] * coefs
    base_rows = lax.dynamic_update_slice(
        jnp.zeros((leaf_size, target_width), jnp.float32), base, (col_pos * share_rows, 0)
    )
    groups = [[0]]
    for reach in range(1, band_reach + 1):
        groups.append([-reach, reach])
    partial = base_rows
    for group in groups:
        kernel = jnp.concatenate([kernel_of(offset) for offset in group], axis=1)
        group_coefs = jnp.concatenate([fetched[offset][:, features:] for offset in group], axis=0)
        partial = partial - mm(kernel, group_coefs)
    bit = 0
    pieces = partial.reshape(leaf_size, target_width)
    while 1 << bit < col_count:
        width = col_width << bit
        view = pieces.reshape(leaf_size, -1, 2, col_width)
        side = (col_pos >> bit) % 2
        keep = lax.dynamic_slice_in_dim(view, side, 1, 2).reshape(leaf_size, -1)
        give = lax.dynamic_slice_in_dim(view, 1 - side, 1, 2).reshape(leaf_size, -1)
        pieces = keep + partner_of(give, "col", 1 << bit)
        bit += 1
    residual = pieces

    current = mm(up_map, residual)
    stacks = []
    for number, (children, low, offset, slice_count) in enumerate(levels):
        ordered = exchange(current, "leaf", leaf_pos, low, children)
        if number == 0:
            group_base = leaf_pos // children * children
            slots = lax.dynamic_slice_in_dim(leaf_map, group_base, children, 0) - group_base
            picked = []
            for slot in range(children):
                piece = ordered[0]
                for source in range(1, children):
                    piece = jnp.where(slots[slot] == source, ordered[source], piece)
                picked.append(piece)
            ordered = picked
        stacked = jnp.concatenate(ordered, axis=0)
        stacks.append(stacked)
        if number < len(levels) - 1:
            current = mm(shared[number][1], stacked)
    values = None
    for number in range(len(levels) - 1, -1, -1):
        own_inv, merge, lift = shared[number]
        fresh_values = mm(own_inv, stacks[number])
        values = fresh_values if values is None else fresh_values - mm_t(lift, values)
    children = levels[0][0]
    local_index = leaf_pos % children
    raw = exchange_raw(values, "leaf", 0, children)
    own_slot = jnp.sum(jnp.arange(children, dtype=jnp.int32) * (slots == local_index))
    incoming = raw[0]
    for m in range(1, children):
        incoming = jnp.where(own_slot == local_index ^ m, raw[m], incoming)

    residual_rows = to_rows(residual, col_pos, col_count)
    solved = mm_t(spread, mm(solve, mm(spread, residual)))
    step = solved - mm(down_map, incoming)
    fresh_rows = coefs + to_rows(step, col_pos, col_count)
    return (residual_rows, fresh_rows)


def solution(mesh):
    return jax.shard_map(
        local,
        mesh=mesh,
        in_specs=(
            P(("leaf", "col"), None),
            P(("leaf", "col"), None),
            P(("leaf", "col"), None),
            P(),
            P("leaf", None),
            P("leaf", None),
            P(),
            P("leaf", None, None),
            P("leaf", None, None),
            P("leaf", None, None),
            P("leaf", None, None),
        ),
        out_specs=(P(("leaf", "col"), None), P(("leaf", "col"), None)),
        check_vma=False,
    )
```

time: 261 us -> 200 us (0.77)
  waiting for transfers between devices: 118 us -> 20.5 us
  local copies, waits for them, and re-layouts: 44.2 us -> 22.9 us
  blocking collectives: 8.86 us -> 26.9 us
  matrix products: 31.4 us -> 43.8 us
  starting transfers between devices: 27.7 us -> 37.3 us
  between operations: 18.7 us -> 28.2 us
  other arithmetic: 11.2 us -> 19 us
    all_gather x4 -> x1, waiting for transfers between devices: 32.7 us -> 0.01 us  [local(): lax.all_gather(jnp.concatenate([part_merge, part_lift], axis=1), 'col', a...]
    reduce_scatter x1 -> x0, waiting for transfers between devices: 26.5 us -> none  [local(): lax.psum_scatter(tile_total, 'col', scatter_dimension=1, tiled=True)]
    gather x6 -> x0, local copies, waits for them, and re-layouts: 25 us -> none  [the longest x1 6.89 us: local(): ordered_a = gathered[1][cluster_order]]
    ppermute x11 -> x23, waiting for transfers between devices: 40.8 us -> 20.5 us  [partner_of(): return lax.ppermute(block, axis, swap_route(lax.axis_size(axis), mask))]
    dot_general x12 -> x23, matrix products: 24.4 us -> 43.8 us  [the longest x13 26.3 us: mm(): return jnp.dot(a, b, precision=high)]
    all_gather x1 -> x2, blocking collectives: 8.86 us -> 26.9 us  [the longest x1 19.5 us: local(): every = lax.all_gather(mine, 'col', axis=1, tiled=True)]
    ppermute x4, waiting for transfers between devices: 16.2 us -> 0.01 us  [shifted(): lax.ppermute(value, axis, [(source, source + steps) for source in range(i...]
    ppermute x11 -> x23, starting transfers between devices: 16 us -> 23 us  [partner_of(): return lax.ppermute(block, axis, swap_route(lax.axis_size(axis), mask))]
  transfers between devices with their start and end apart: 20 -> 28, of which waited for: 13 -> 9; matrix products, arithmetic and copies ran while one was open for 25% -> 39% of each run, Pallas kernels for 0% -> 0%
where the time goes in v1:
time: 200 us; the launch traced here: 199 us
  matrix products  43.8 us (22%)
  starting transfers between devices  37.3 us (19%)
  between operations  28.2 us (14%)
  blocking collectives  26.9 us (13%)
  local copies, waits for them, and re-layouts  22.9 us (11%)
  waiting for transfers between devices  20.5 us (10%)
  other arithmetic  19 us (10%)
    dot_general x13, matrix products, mm(): return jnp.dot(a, b, precision=high)  26.3 us
    ppermute x23, starting transfers between devices, partner_of(): return lax.ppermute(block, axis, swap_route(lax.axis_size(axis), mask))  23 us
    ppermute x23, waiting for transfers between devices, partner_of(): return lax.ppermute(block, axis, swap_route(lax.axis_size(axis), mask))  20.5 us
    all_gather x1, blocking collectives, local(): every = lax.all_gather(mine, 'col', axis=1, tiled=True)  19.5 us
    ppermute x4, starting transfers between devices, shifted(): lax.ppermute(value, axis, [(source, source + steps) for source in range(i...  14.3 us
    dot_general x4, matrix products, mm_t(): return jnp.einsum('ka,kc->ac', a, b, precision=high)  10.8 us
    all_gather x1, blocking collectives, local(): rows_x = lax.all_gather(points, 'col', axis=0, tiled=True)  7.4 us
    dot_general x5, matrix products, kernel_of(): inner = jnp.einsum('pf,qf->pq', rows_x, column_points, precision=high)  6.15 us
  transfers between devices with their start and end apart: 28, of which 9 were waited for; matrix products, arithmetic and copies ran while one was open for 39% of the time, Pallas kernels for 0%

profile of v1, /device:TPU:0, one launch (start us, length us, event | category | flops | bytes accessed | tf_op | source)
XLA Modules:
  0.0 198.7 jit_solution(7557876273023577676)
XLA Ops:
  7.3 1.7 multiply_reduce_fusion.5
  9.0 2.0 constant_dynamic-update-slice_fusion
  12.2 6.3 %collective-permute-start = (f32[256,640]{1,0:T(8,128)}, f32[256,640]{1,0:T(8,128)}, u32[]{:S(2)}, u32[]{:S(2)}) collective-permute-start(f32[256,640]{1,0:T(8,128)} %constant_dynamic-update-slice_fusion), channel_id=1, source_target_pairs={{0,4},{4,8},{8,12},{12,16},{16,20},{20,24},{24,28},{1,5},{5,9},{9,... | collective-permute-start | bytes 1966088 | tf_op jit(solution)/shard_map/ppermute | solution.py:20
  19.9 5.4 %collective-permute-start.2 = (f32[256,640]{1,0:T(8,128)}, f32[256,640]{1,0:T(8,128)}, u32[]{:S(2)}, u32[]{:S(2)}) collective-permute-start(f32[256,640]{1,0:T(8,128)} %constant_dynamic-update-slice_fusion), channel_id=1, source_target_pairs={{0,8},{4,12},{8,16},{12,20},{16,24},{20,28},{1,9},{5,13},{9,17},{1... | collective-permute-start | bytes 1966088 | tf_op jit(solution)/shard_map/ppermute | solution.py:20
  26.9 2.2 %collective-permute-start.17 = (f32[1,16,512]{2,1,0:T(8,128)}, f32[1,16,512]{2,1,0:T(8,128)}, u32[]{:S(2)}, u32[]{:S(2)}) collective-permute-start(f32[1,16,512]{2,1,0:T(8,128)} %constant_dynamic-slice_fusion.2), channel_id=1, source_target_pairs={{0,12},{4,8},{8,4},{12,0},{16,28},{20,24},{24,20},{28,16},{1,13},{... | collective-permute-start | bytes 98312 | tf_op jit(solution)/shard_map/ppermute | solution.py:14
  29.1 7.4 %all_gather.9 = f32[1024,128]{1,0:T(8,128)S(1)} all-gather(f32[256,128]{1,0:T(8,128)} %param.11), channel_id=1, replica_groups=mesh['leaf'=8,'col'=4] {'col'}, dimensions={0}, use_global_device_ids=true | all-gather | bytes 655360 | tf_op jit(solution)/shard_map/all_gather | solution.py:106
  41.5 2.4 %fusion.88 = f32[1024,512]{0,1:T(8,128)} fusion(f32[1024,256]{1,0:T(8,128)S(1)} %fusion.31, f32[256,512]{1,0:T(8,128)S(1)} %copy-done.2), kind=kOutput, calls=%fused_computation.163 | convolution fusion | flops 805306368 | bytes 3670016 | tf_op jit(solution)/shard_map/dot_general | solution.py:57
  43.8 4.0 %fusion.2 = f32[1024,256]{1,0:T(8,128)S(1)} fusion(f32[1,1024,1024]{2,1,0:T(8,128)} %param.18, f32[1,1024,256]{2,1,0:T(8,128)S(1)} %copy-done), kind=kOutput, calls=%fused_computation.2 | convolution fusion | flops 1610612736 | bytes 6291456 | tf_op jit(solution)/shard_map/dot_general | solution.py:57
  47.9 3.5 %fusion.7 = f32[1024,256]{1,0:T(8,128)} fusion(f32[1024,256]{1,0:T(8,128)S(1)} %fusion.2, s32[1024]{0:T(1024)S(1)} %bitcast.96), kind=kOutput, calls=%fused_computation.8 | convolution fusion | flops 1611661312 | bytes 2101248 | tf_op jit(solution)/shard_map/ka,kc->ac/dot_general | solution.py:61
  53.0 2.0 subtract_dynamic-update-slice_fusion
  55.0 2.1 %fusion.46 = f32[64,1024]{1,0:T(8,128)} fusion(f32[1,320,1024]{2,1,0:T(8,128)S(1)} %copy-done.4, f32[1,320,256]{2,1,0:T(8,128)} %param.21, s32[]{:T(128)S(6)} %select_n.416), kind=kOutput, calls=%fused_computation.51 | convolution fusion | flops 100663296 | bytes 1441796 | tf_op jit(solution)/shard_map/dot_general | solution.py:57
  57.1 1.7 dynamic-slice_bitcast_fusion
  62.0 4.1 %fusion = f32[256,1024]{1,0:T(8,128)S(1)} fusion(f32[1,1024,1024]{2,1,0:T(8,128)} %param.18, f32[1,1024,256]{2,1,0:T(8,128)S(1)} %copy-done), kind=kOutput, calls=%fused_computation | convolution fusion | flops 1610612736 | bytes 6291456 | tf_op jit(solution)/shard_map/ka,kc->ac/dot_general | solution.py:61
  77.2 2.1 %fusion.12 = f32[1024,512]{0,1:T(8,128)S(1)} fusion(f32[1024,256]{1,0:T(8,128)S(1)} %exponential_select_fusion.2, f32[1024,256]{1,0:T(8,128)S(1)} %exponential_select_fusion.3, f32[256,512]{1,0:T(8,128)S(1)} %slice.95, f32[256,512]{1,0:T(8,128)S(1)} %slice.94), kind=kOutput, calls=%fused_computation.12 | convolution fusion | flops 1611399168 | bytes 5242880 | tf_op jit(solution)/shard_map/dot_general | solution.py:57
  82.2 1.6 exponential_select_fusion.1
  83.9 3.6 %subtract_subtract_fusion = f32[1024,512]{0,1:T(8,128)S(1)} fusion(f32[1024,512]{0,1:T(8,128)S(1)} %fusion.12, f32[1024,512]{0,1:T(8,128)} %subtract_dynamic-update-slice_fusion, f32[1024,512]{0,1:T(8,128)S(1)} %copy-done.3, f32[1024,256]{1,0:T(8,128)S(1)} %exponential_select_fusion, f32[1024,256]{1,0:T(8,128)S(1)} %exponential_select_fusion.1, ...), kind=kOutput, calls=%fused_computation.24 | convolution fusion | flops 1612972032 | bytes 11534336 | tf_op jit(solution)/shard_map/dot_general | solution.py:57
  88.9 2.7 %fusion.6 = f32[256,1024]{1,0:T(8,128)} fusion(f32[256,1024]{1,0:T(8,128)S(1)} %fusion, s32[1024]{0:T(1024)S(1)} %bitcast.97), kind=kOutput, calls=%fused_computation.7 | convolution fusion | flops 1611661312 | bytes 2101248 | tf_op jit(solution)/shard_map/dot_general | solution.py:57
  102.3 1.7 collective-permute-start.15
  113.3 3.0 %collective-permute-done.13 = f32[64,1024]{1,0:T(8,128)S(1)} collective-permute-done((f32[64,1024]{1,0:T(8,128)S(1)}, f32[64,1024]{1,0:T(8,128)S(1)}, u32[]{:S(2)}, u32[]{:S(2)}) %collective-permute-start.13) | collective-permute-done | bytes 262176 | tf_op jit(solution)/shard_map/ppermute | solution.py:14
  121.2 1.7 pad_maximum_fusion.1
  123.7 19.5 %all_gather.11 = f32[4,64,512]{2,1,0:T(8,128)S(1)} all-gather(f32[4,16,512]{2,1,0:T(8,128)S(1)} %pad_maximum_fusion.4), channel_id=1, replica_groups=mesh['leaf'=8,'col'=4] {'col'}, dimensions={1}, use_global_device_ids=true | all-gather | bytes 655360 | tf_op jit(solution)/shard_map/all_gather | solution.py:136
  143.2 2.1 %copy.25 = f32[1024,1,1,128]{3,0,2,1:T(8,128)} copy(f32[1024,1,1,128]{0,3,2,1:T(8,128)} %get-tuple-element.11) | data formatting | bytes 1048576 | tf_op jit(solution)/shard_map/dynamic_slice | solution.py:178
  147.4 2.5 %collective-permute-start.9 = (f32[256,128]{1,0:T(8,128)S(1)}, f32[256,128]{1,0:T(8,128)S(1)}, u32[]{:S(2)}, u32[]{:S(2)}) collective-permute-start(f32[256,128]{1,0:T(8,128)S(1)} %fusion.89), channel_id=1, source_target_pairs={{0,4},{4,0},{8,12},{12,8},{16,20},{20,16},{24,28},{28,24},{1,5},{5... | collective-permute-start | bytes 393224 | tf_op jit(solution)/shard_map/ppermute | solution.py:14
  155.5 3.2 %fusion.4 = f32[128,1024]{1,0:T(8,128)} fusion(f32[1024,128]{1,0:T(8,128)S(1)} %fusion.9, f32[1,1024,1024]{2,1,0:T(8,128)S(1)} %copy-done.1), kind=kOutput, calls=%fused_computation.4 | convolution fusion | flops 805306368 | bytes 5242880 | tf_op jit(solution)/shard_map/dot_general | solution.py:57
  159.5 1.9 fusion.32
  162.7 1.6 convolution_bitcast_fusion
  164.3 5.7 %collective-permute-done.20 = f32[256,128]{1,0:T(8,128)S(1)} collective-permute-done((f32[256,128]{1,0:T(8,128)S(1)}, f32[256,128]{1,0:T(8,128)S(1)}, u32[]{:S(2)}, u32[]{:S(2)}) %collective-permute-start.20) | collective-permute-done | bytes 131104 | tf_op jit(solution)/shard_map/ppermute | solution.py:14
  171.8 2.9 %collective-permute-start.22 = (f32[256,128]{0,1:T(8,128)S(1)}, f32[256,128]{0,1:T(8,128)S(1)}, u32[]{:S(2)}, u32[]{:S(2)}) collective-permute-start(f32[256,128]{0,1:T(8,128)S(1)} %convolution_subtract_fusion.1), channel_id=1, source_target_pairs={{0,8},{4,12},{8,0},{12,4},{16,24},{20,28},{24,16},{28,20},{1,9},{5... | collective-permute-start | bytes 393224 | tf_op jit(solution)/shard_map/ppermute | solution.py:14
  175.2 1.9 fusion.10
  179.0 1.9 collective-permute-done.22
  184.6 4.3 %collective-permute-done.25 = f32[256,128]{1,0:T(8,128)S(1)} collective-permute-done((f32[256,128]{1,0:T(8,128)S(1)}, f32[256,128]{1,0:T(8,128)S(1)}, u32[]{:S(2)}, u32[]{:S(2)}) %collective-permute-start.25) | collective-permute-done | bytes 131104 | tf_op jit(solution)/shard_map/ppermute | solution.py:14
  189.0 2.0 collective-permute-done.26
  (146 shorter events, 59.8 us)
Async XLA Ops:
  7.2 36.7 %copy-start = (f32[1,1024,256]{2,1,0:T(8,128)S(1)}, f32[1,1024,256]{2,1,0:T(8,128)}, u32[]{:S(2)}) copy-start(f32[1,1024,256]{2,1,0:T(8,128)} %param.19) | copy-start | bytes 3145732
  7.2 30.6 %copy-start.21 = (s32[1,5]{1,0:T(1,128)S(1)}, s32[1,5]{1,0:T(1,128)}, u32[]{:S(2)}) copy-start(s32[1,5]{1,0:T(1,128)} %param.15) | copy-start | bytes 64
  7.2 31.2 %copy-start.17 = (f32[256,512]{1,0:T(8,128)S(1)}, f32[256,512]{1,0:T(8,128)}, u32[]{:S(2)}) copy-start(f32[256,512]{1,0:T(8,128)} %param.13) | copy-start | bytes 1572868
  7.2 152.3 %all-gather.2.cloned.1.call-start = ((), (), s32[]{:S(2)}) async-start(), calls=%async_computation | async-start | bytes 1638400 | tf_op jit(solution)/shard_map/all_gather | solution.py:153
  9.0 31.8 %copy-start.13 = (f32[256,128]{1,0:T(8,128)S(1)}, f32[256,128]{1,0:T(8,128)}, u32[]{:S(2)}) copy-start(f32[256,128]{1,0:T(8,128)} %param.11) | copy-start | bytes 393220
  10.9 55.2 %collective-permute-start.1 = (f32[256,640]{1,0:T(8,128)}, f32[256,640]{1,0:T(8,128)}, u32[]{:S(2)}, u32[]{:S(2)}) collective-permute-start(f32[256,640]{1,0:T(8,128)} %constant_dynamic-update-slice_fusion), channel_id=1, source_target_pairs={{4,0},{8,4},{12,8},{16,12},{20,16},{24,20},{28,24},{5,1},{9,5},{13... | collective-permute-start | bytes 1966088 | tf_op jit(solution)/shard_map/ppermute | solution.py:20
  12.2 56.3 %collective-permute-start = (f32[256,640]{1,0:T(8,128)}, f32[256,640]{1,0:T(8,128)}, u32[]{:S(2)}, u32[]{:S(2)}) collective-permute-start(f32[256,640]{1,0:T(8,128)} %constant_dynamic-update-slice_fusion), channel_id=1, source_target_pairs={{0,4},{4,8},{8,12},{12,16},{16,20},{20,24},{24,28},{1,5},{5,9},{9,... | collective-permute-start | bytes 1966088 | tf_op jit(solution)/shard_map/ppermute | solution.py:20
  18.6 53.6 %collective-permute-start.3 = (f32[256,640]{1,0:T(8,128)}, f32[256,640]{1,0:T(8,128)S(1)}, u32[]{:S(2)}, u32[]{:S(2)}) collective-permute-start(f32[256,640]{1,0:T(8,128)} %constant_dynamic-update-slice_fusion), channel_id=1, source_target_pairs={{8,0},{12,4},{16,8},{20,12},{24,16},{28,20},{9,1},{13,5},{17,9},{2... | collective-permute-start | bytes 1966088 | tf_op jit(solution)/shard_map/ppermute | solution.py:20
  19.9 59.4 %collective-permute-start.2 = (f32[256,640]{1,0:T(8,128)}, f32[256,640]{1,0:T(8,128)}, u32[]{:S(2)}, u32[]{:S(2)}) collective-permute-start(f32[256,640]{1,0:T(8,128)} %constant_dynamic-update-slice_fusion), channel_id=1, source_target_pairs={{0,8},{4,12},{8,16},{12,20},{16,24},{20,28},{1,9},{5,13},{9,17},{1... | collective-permute-start | bytes 1966088 | tf_op jit(solution)/shard_map/ppermute | solution.py:20
  26.9 75.2 %collective-permute-start.17 = (f32[1,16,512]{2,1,0:T(8,128)}, f32[1,16,512]{2,1,0:T(8,128)}, u32[]{:S(2)}, u32[]{:S(2)}) collective-permute-start(f32[1,16,512]{2,1,0:T(8,128)} %constant_dynamic-slice_fusion.2), channel_id=1, source_target_pairs={{0,12},{4,8},{8,4},{12,0},{16,28},{20,24},{24,20},{28,16},{1,13},{... | collective-permute-start | bytes 98312 | tf_op jit(solution)/shard_map/ppermute | solution.py:14
  66.1 36.2 %collective-permute-start.18 = (f32[1,16,512]{2,1,0:T(8,128)}, f32[1,16,512]{2,1,0:T(8,128)}, u32[]{:S(2)}, u32[]{:S(2)}) collective-permute-start(f32[1,16,512]{2,1,0:T(8,128)} %constant_dynamic-slice_fusion.2), channel_id=1, source_target_pairs={{0,8},{4,12},{8,0},{12,4},{16,24},{20,28},{24,16},{28,20},{1,9},{5... | collective-permute-start | bytes 98312 | tf_op jit(solution)/shard_map/ppermute | solution.py:14
  68.6 35.5 %collective-permute-start.19 = (f32[1,16,512]{2,1,0:T(8,128)}, f32[1,16,512]{2,1,0:T(8,128)}, u32[]{:S(2)}, u32[]{:S(2)}) collective-permute-start(f32[1,16,512]{2,1,0:T(8,128)} %constant_dynamic-slice_fusion.2), channel_id=1, source_target_pairs={{0,4},{4,0},{8,12},{12,8},{16,20},{20,16},{24,28},{28,24},{1,5},{5... | collective-permute-start | bytes 98312 | tf_op jit(solution)/shard_map/ppermute | solution.py:14
  72.2 34.8 %collective-permute-start.12 = (f32[64,1024]{1,0:T(8,128)}, f32[64,1024]{1,0:T(8,128)}, u32[]{:S(2)}, u32[]{:S(2)}) collective-permute-start(f32[64,1024]{1,0:T(8,128)} %fusion.46), channel_id=1, source_target_pairs={{0,4},{4,0},{8,12},{12,8},{16,20},{20,16},{24,28},{28,24},{1,5},{5... | collective-permute-start | bytes 786440 | tf_op jit(solution)/shard_map/ppermute | solution.py:14
  88.9 28.2 %collective-permute-start.4 = (f32[1024,256]{0,1:T(8,128)}, f32[1024,256]{0,1:T(8,128)}, u32[]{:S(2)}, u32[]{:S(2)}) collective-permute-start(f32[1024,256]{0,1:T(8,128)} %bitcast.12), channel_id=1, source_target_pairs={{0,1},{1,0},{2,3},{3,2},{4,5},{5,4},{6,7},{7,6},{8,9},{9,8},{10,11... | collective-permute-start | bytes 3145736 | tf_op jit(solution)/shard_map/ppermute | solution.py:14
  102.1 7.3 %collective-permute-start.14 = (f32[64,256]{0,1:T(8,128)S(1)}, f32[64,256]{0,1:T(8,128)S(1)}, u32[]{:S(2)}, u32[]{:S(2)}) collective-permute-start(f32[64,256]{0,1:T(8,128)S(1)} %copy-done.19), channel_id=1, source_target_pairs={{0,12},{4,8},{8,4},{12,0},{16,28},{20,24},{24,20},{28,16},{1,13},{... | collective-permute-start | bytes 196616 | tf_op jit(solution)/shard_map/ppermute | solution.py:14
  102.3 8.6 %collective-permute-start.15 = (f32[64,256]{0,1:T(8,128)S(1)}, f32[64,256]{0,1:T(8,128)S(1)}, u32[]{:S(2)}, u32[]{:S(2)}) collective-permute-start(f32[64,256]{0,1:T(8,128)S(1)} %copy-done.19), channel_id=1, source_target_pairs={{0,8},{4,12},{8,0},{12,4},{16,24},{20,28},{24,16},{28,20},{1,9},{5... | collective-permute-start | bytes 196616 | tf_op jit(solution)/shard_map/ppermute | solution.py:14
  104.1 7.7 %collective-permute-start.16 = (f32[64,256]{0,1:T(8,128)S(1)}, f32[64,256]{0,1:T(8,128)S(1)}, u32[]{:S(2)}, u32[]{:S(2)}) collective-permute-start(f32[64,256]{0,1:T(8,128)S(1)} %copy-done.19), channel_id=1, source_target_pairs={{0,4},{4,0},{8,12},{12,8},{16,20},{20,16},{24,28},{28,24},{1,5},{5... | collective-permute-start | bytes 196616 | tf_op jit(solution)/shard_map/ppermute | solution.py:14
  108.2 8.1 %collective-permute-start.13 = (f32[64,1024]{1,0:T(8,128)S(1)}, f32[64,1024]{1,0:T(8,128)S(1)}, u32[]{:S(2)}, u32[]{:S(2)}) collective-permute-start(f32[64,1024]{1,0:T(8,128)S(1)} %add.193), channel_id=1, source_target_pairs={{0,8},{4,12},{8,0},{12,4},{16,24},{20,28},{24,16},{28,20},{1,9},{5... | collective-permute-start | bytes 786440 | tf_op jit(solution)/shard_map/ppermute | solution.py:14
  120.3 24.9 %collective-permute-start.5 = (f32[1024,128]{1,0:T(8,128)}, f32[1024,128]{1,0:T(8,128)}, u32[]{:S(2)}, u32[]{:S(2)}) collective-permute-start(f32[1024,128]{1,0:T(8,128)} %bitcast.95), channel_id=1, source_target_pairs={{0,2},{1,3},{2,0},{3,1},{4,6},{5,7},{6,4},{7,5},{8,10},{9,11},{10,... | collective-permute-start | bytes 1572872 | tf_op jit(solution)/shard_map/ppermute | solution.py:14
  147.4 11.3 %collective-permute-start.9 = (f32[256,128]{1,0:T(8,128)S(1)}, f32[256,128]{1,0:T(8,128)S(1)}, u32[]{:S(2)}, u32[]{:S(2)}) collective-permute-start(f32[256,128]{1,0:T(8,128)S(1)} %fusion.89), channel_id=1, source_target_pairs={{0,4},{4,0},{8,12},{12,8},{16,20},{20,16},{24,28},{28,24},{1,5},{5... | collective-permute-start | bytes 393224 | tf_op jit(solution)/shard_map/ppermute | solution.py:14
  149.9 8.8 %collective-permute-start.11 = (f32[256,128]{1,0:T(8,128)S(1)}, f32[256,128]{1,0:T(8,128)S(1)}, u32[]{:S(2)}, u32[]{:S(2)}) collective-permute-start(f32[256,128]{1,0:T(8,128)S(1)} %fusion.89), channel_id=1, source_target_pairs={{0,12},{4,8},{8,4},{12,0},{16,28},{20,24},{24,20},{28,16},{1,13},{... | collective-permute-start | bytes 393224 | tf_op jit(solution)/shard_map/ppermute | solution.py:14
  149.9 8.8 %collective-permute-start.10 = (f32[256,128]{1,0:T(8,128)S(1)}, f32[256,128]{1,0:T(8,128)S(1)}, u32[]{:S(2)}, u32[]{:S(2)}) collective-permute-start(f32[256,128]{1,0:T(8,128)S(1)} %fusion.89), channel_id=1, source_target_pairs={{0,8},{4,12},{8,0},{12,4},{16,24},{20,28},{24,16},{28,20},{1,9},{5... | collective-permute-start | bytes 393224 | tf_op jit(solution)/shard_map/ppermute | solution.py:14
  152.3 24.9 %collective-permute-start.6 = (f32[256,128]{1,0:T(8,128)}, f32[256,128]{1,0:T(8,128)}, u32[]{:S(2)}, u32[]{:S(2)}) collective-permute-start(f32[256,128]{1,0:T(8,128)} %get-tuple-element.26), channel_id=1, source_target_pairs={{0,1},{1,0},{2,3},{3,2},{4,5},{5,4},{6,7},{7,6},{8,9},{9,8},{10,11... | collective-permute-start | bytes 393224 | tf_op jit(solution)/shard_map/ppermute | solution.py:14
  153.1 28.6 %collective-permute-start.7 = (f32[256,128]{1,0:T(8,128)}, f32[256,128]{1,0:T(8,128)}, u32[]{:S(2)}, u32[]{:S(2)}) collective-permute-start(f32[256,128]{1,0:T(8,128)} %get-tuple-element.25), channel_id=1, source_target_pairs={{0,2},{1,3},{2,0},{3,1},{4,6},{5,7},{6,4},{7,5},{8,10},{9,11},{10,... | collective-permute-start | bytes 393224 | tf_op jit(solution)/shard_map/ppermute | solution.py:14
  161.4 8.6 %collective-permute-start.20 = (f32[256,128]{1,0:T(8,128)S(1)}, f32[256,128]{1,0:T(8,128)S(1)}, u32[]{:S(2)}, u32[]{:S(2)}) collective-permute-start(f32[256,128]{1,0:T(8,128)S(1)} %fusion.32), channel_id=1, source_target_pairs={{0,16},{4,20},{8,24},{12,28},{16,0},{20,4},{24,8},{28,12},{1,17},{... | collective-permute-start | bytes 393224 | tf_op jit(solution)/shard_map/ppermute | solution.py:14
  171.7 7.3 %collective-permute-start.21 = (f32[256,128]{0,1:T(8,128)S(1)}, f32[256,128]{0,1:T(8,128)S(1)}, u32[]{:S(2)}, u32[]{:S(2)}) collective-permute-start(f32[256,128]{0,1:T(8,128)S(1)} %convolution_subtract_fusion.1), channel_id=1, source_target_pairs={{0,12},{4,8},{8,4},{12,0},{16,28},{20,24},{24,20},{28,16},{1,13},{... | collective-permute-start | bytes 393224 | tf_op jit(solution)/shard_map/ppermute | solution.py:14
  171.8 9.1 %collective-permute-start.22 = (f32[256,128]{0,1:T(8,128)S(1)}, f32[256,128]{0,1:T(8,128)S(1)}, u32[]{:S(2)}, u32[]{:S(2)}) collective-permute-start(f32[256,128]{0,1:T(8,128)S(1)} %convolution_subtract_fusion.1), channel_id=1, source_target_pairs={{0,8},{4,12},{8,0},{12,4},{16,24},{20,28},{24,16},{28,20},{1,9},{5... | collective-permute-start | bytes 393224 | tf_op jit(solution)/shard_map/ppermute | solution.py:14
  174.7 6.2 %collective-permute-start.23 = (f32[256,128]{0,1:T(8,128)S(1)}, f32[256,128]{0,1:T(8,128)S(1)}, u32[]{:S(2)}, u32[]{:S(2)}) collective-permute-start(f32[256,128]{0,1:T(8,128)S(1)} %convolution_subtract_fusion.1), channel_id=1, source_target_pairs={{0,4},{4,0},{8,12},{12,8},{16,20},{20,16},{24,28},{28,24},{1,5},{5... | collective-permute-start | bytes 393224 | tf_op jit(solution)/shard_map/ppermute | solution.py:14
  177.2 6.5 %collective-permute-start.8 = (f32[256,128]{1,0:T(8,128)S(1)}, f32[256,128]{1,0:T(8,128)S(1)}, u32[]{:S(2)}, u32[]{:S(2)}) collective-permute-start(f32[256,128]{1,0:T(8,128)S(1)} %copy-done.20), channel_id=1, source_target_pairs={{0,3},{1,2},{2,1},{3,0},{4,7},{5,6},{6,5},{7,4},{8,11},{9,10},{10,... | collective-permute-start | bytes 393224 | tf_op jit(solution)/shard_map/ppermute | solution.py:14
  181.6 3.0 %collective-permute-start.24 = (f32[256,128]{1,0:T(8,128)S(1)}, f32[256,128]{1,0:T(8,128)S(1)}, u32[]{:S(2)}, u32[]{:S(2)}) collective-permute-start(f32[256,128]{1,0:T(8,128)S(1)} %get-tuple-element.15), channel_id=1, source_target_pairs={{0,1},{1,0},{2,3},{3,2},{4,5},{5,4},{6,7},{7,6},{8,9},{9,8},{10,11... | collective-permute-start | bytes 393224 | tf_op jit(solution)/shard_map/ppermute | solution.py:14
  182.6 6.4 %collective-permute-start.25 = (f32[256,128]{1,0:T(8,128)S(1)}, f32[256,128]{1,0:T(8,128)S(1)}, u32[]{:S(2)}, u32[]{:S(2)}) collective-permute-start(f32[256,128]{1,0:T(8,128)S(1)} %get-tuple-element.14), channel_id=1, source_target_pairs={{0,2},{1,3},{2,0},{3,1},{4,6},{5,7},{6,4},{7,5},{8,10},{9,11},{10,... | collective-permute-start | bytes 393224 | tf_op jit(solution)/shard_map/ppermute | solution.py:14
  183.7 7.3 %collective-permute-start.26 = (f32[256,128]{1,0:T(8,128)S(1)}, f32[256,128]{1,0:T(8,128)S(1)}, u32[]{:S(2)}, u32[]{:S(2)}) collective-permute-start(f32[256,128]{1,0:T(8,128)S(1)} %get-tuple-element.13), channel_id=1, source_target_pairs={{0,3},{1,2},{2,1},{3,0},{4,7},{5,6},{6,5},{7,4},{8,11},{9,10},{10,... | collective-permute-start | bytes 393224 | tf_op jit(solution)/shard_map/ppermute | solution.py:14
  (21 other events, 185.5 us)
Sparse Core Ops, SparseCore 0:
  123.0 21.6 all-gather.1

commit v2 on v1

--- a/solution.py
+++ b/solution.py
@@ -1,6 +1,10 @@
+import functools
+
 import jax
 import jax.numpy as jnp
 from jax import lax
+from jax.experimental import pallas as pl
+from jax.experimental.pallas import tpu as pltpu
 from jax.sharding import PartitionSpec as P
 
 high = lax.Precision.HIGH
@@ -72,6 +76,102 @@
             piece = partner_of(piece, "col", m)
         out = lax.dynamic_update_slice(out, piece, (0, target * width))
     return out
+
+
+def halves(value):
+    top = value.astype(jnp.bfloat16)
+    return top, (value - top.astype(jnp.float32)).astype(jnp.bfloat16)
+
+
+def product(left, right, contract):
+    def one(a, b):
+        return lax.dot_general(a, b, (contract, ((), ())), preferred_element_type=jnp.float32)
+
+    return one(left[0], right[0]) + (one(left[0], right[1]) + one(left[1], right[0]))
+
+
+def band_body(count, features, cols, *refs):
+    mask_ref, ridge_ref, pos_ref, rows_ref, targets_ref = refs[:5]
+    fetched = refs[5 : 5 + count]
+    outs = refs[5 + count : 5 + count + cols]
+    x_top, x_low, a_top, a_low, squares = refs[5 + count + cols :]
+    step = pl.program_id(0)
+    share = targets_ref.shape[0]
+    flat = ((1,), (1,))
+
+    @pl.when(step == 0)
+    def _():
+        ones = jnp.ones((8, features), jnp.bfloat16)
+        for k in range(count):
+            span = pl.ds(k * share, share)
+            x = fetched[k][:, :features]
+            x_top[span, :], x_low[span, :] = halves(x)
+            a_top[span, :], a_low[span, :] = halves(fetched[k][:, features:])
+            first, rest = halves(x * x)
+            last = (x * x - first.astype(jnp.float32) - rest.astype(jnp.float32)).astype(
+                jnp.bfloat16
+            )
+            total = jnp.zeros((8, share), jnp.float32)
+            for part in (last, rest, first):
+                total += lax.dot_general(
+                    ones, part, (flat, ((), ())), preferred_element_type=jnp.float32
+                )
+            squares[:, span] = total
+
+    rows = rows_ref[...]
+    row_squares = jnp.sum(rows * rows, axis=1, keepdims=True)
+    row_halves = halves(rows)
+    own = fetched[count // 2][:, features:]
+    base = targets_ref[...] - ridge_ref[0] * own
+    total = jnp.where(step == pos_ref[0], base, jnp.zeros_like(base))
+    for k in range(count):
+        span = pl.ds(k * share, share)
+        inner = product(row_halves, (x_top[span, :], x_low[span, :]), flat)
+        distance = row_squares + squares[0:1, span] - 2.0 * inner
+        kernel = jnp.exp(distance * (-2.0 / features))
+        kernel = jnp.where(mask_ref[0, k] > 0, kernel, jnp.zeros_like(kernel))
+        total -= product(halves(kernel), (a_top[span, :], a_low[span, :]), ((1,), (0,)))
+    width = total.shape[1] // cols
+    pieces = [total[:, m * width : (m + 1) * width] for m in range(cols)]
+    bit = 0
+    while 1 << bit < cols:
+        odd = (pos_ref[0] >> bit) % 2 == 1
+        pieces = [jnp.where(odd, pieces[m ^ (1 << bit)], pieces[m]) for m in range(cols)]
+        bit += 1
+    for out, piece in zip(outs, pieces):
+        out[...] = piece
+
+
+def band_products(rows_x, fetched, targets, ridge, tile_mask, col_pos, cols):
+    leaf_size, features = rows_x.shape
+    share, wide = fetched[0].shape
+    target_width = targets.shape[1]
+    width = target_width // cols
+    count = len(fetched)
+    smem = pl.BlockSpec(memory_space=pltpu.SMEM)
+    whole = lambda shape: pl.BlockSpec(shape, lambda i: (0, 0))
+    return pl.pallas_call(
+        functools.partial(band_body, count, features, cols),
+        grid=(leaf_size // share,),
+        in_specs=[smem, smem, smem, pl.BlockSpec((share, features), lambda i: (i, 0))]
+        + [whole((share, target_width))]
+        + [whole((share, wide))] * count,
+        out_specs=[pl.BlockSpec((share, width), lambda i: (i, 0))] * cols,
+        out_shape=[jax.ShapeDtypeStruct((leaf_size, width), jnp.float32)] * cols,
+        scratch_shapes=[
+            pltpu.VMEM((count * share, features), jnp.bfloat16),
+            pltpu.VMEM((count * share, features), jnp.bfloat16),
+            pltpu.VMEM((count * share, target_width), jnp.bfloat16),
+            pltpu.VMEM((count * share, target_width), jnp.bfloat16),
+            pltpu.VMEM((8, count * share), jnp.float32),
+        ],
+        compiler_params=pltpu.CompilerParams(vmem_limit_bytes=40 * 1024 * 1024),
+        cost_estimate=pl.CostEstimate(
+            flops=12 * leaf_size * share * count * wide // 2,
+            bytes_accessed=8 * leaf_size * target_width,
+            transcendentals=leaf_size * share * count,
+        ),
+    )(tile_mask, ridge, jnp.reshape(col_pos, (1,)).astype(jnp.int32), rows_x, targets, *fetched)
 
 
 def local(
@@ -96,90 +196,50 @@
     target_width = coefs.shape[1]
     col_width = target_width // col_count
     band_reach = tile_mask.shape[1] // 2
-    scale = -2.0 / features
 
     packed = jnp.concatenate([points, coefs], axis=1)
-    fetched = {0: packed}
+    fetched = []
     for offset in range(-band_reach, band_reach + 1):
-        if offset != 0:
-            fetched[offset] = shifted(packed, "leaf", -offset)
+        fetched.append(shifted(packed, "leaf", -offset) if offset else packed)
     rows_x = lax.all_gather(points, "col", axis=0, tiled=True)
-    row_squares = jnp.sum(rows_x * rows_x, axis=1)
-
-    def kernel_of(offset):
-        column_points = fetched[offset][:, :features]
-        squares = jnp.sum(column_points * column_points, axis=1)
-        inner = jnp.einsum("pf,qf->pq", rows_x, column_points, precision=high)
-        values = jnp.exp((row_squares[:, None] + squares[None, :] - 2.0 * inner) * scale)
-        return jnp.where(tile_mask[0, offset + band_reach] > 0, values, 0.0)
 
     basis = leaf_basis[0]
     solve = leaf_inverse[0]
     rank_size = basis.shape[1]
     order = cluster_perm[0]
     spread = (order[:, None] == jnp.arange(leaf_size, dtype=jnp.int32)[None, :]).astype(jnp.float32)
-    down_map = mm_t(spread, mm(solve, basis))
     up_map = mm(mm_t(basis, solve), spread)
 
     levels = tree_levels(leaf_count, rank_size)
-    share_rank = rank_size // col_count
     shared = []
     for number, (children, low, offset, slice_count) in enumerate(levels):
         node_rows = children * rank_size
         node_inv = node_inverse[0, offset : offset + slice_count, :node_rows]
-        if number > 0:
-            part = slice_count // col_count
-            mine = lax.dynamic_slice_in_dim(node_inv, col_pos * part, part, 0)[None]
-            for below in range(number):
-                fan, below_low = levels[below][:2]
-                mine = jnp.concatenate(exchange(mine, "leaf", leaf_pos, below_low, fan), axis=0)
-            every = lax.all_gather(mine, "col", axis=1, tiled=True)
-            own_inv = every.reshape(rank_size, node_rows)
-        else:
-            own_inv = node_inv
+        own_inv = node_inv
+        for fan, digit_low in [level[:2] for level in levels[:number]]:
+            own_inv = jnp.concatenate(exchange(own_inv, "leaf", leaf_pos, digit_low, fan), axis=0)
+        transfer = None
         lift = None
-        merge = None
         if number < len(levels) - 1:
-            transfer = lax.dynamic_slice(
-                node_transfer[0], (offset, col_pos * share_rank), (slice_count, share_rank)
-            ).T
-            part_merge = mm(transfer, node_inv)
+            transfer = node_transfer[0, offset : offset + slice_count]
             whole = transfer
             for fan, digit_low in [level[:2] for level in levels[: number + 1]]:
-                whole = jnp.concatenate(exchange(whole, "leaf", leaf_pos, digit_low, fan), axis=1)
-                for bit in range(fan.bit_length() - 1):
-                    part_merge = part_merge + partner_of(part_merge, "leaf", 1 << (digit_low + bit))
-            part_lift = jnp.einsum("ra,ba->rb", whole, own_inv, precision=high)
-            both = lax.all_gather(
-                jnp.concatenate([part_merge, part_lift], axis=1), "col", axis=0, tiled=True
-            )
-            merge = both[:, :node_rows]
-            lift = both[:, node_rows:]
-        shared.append((own_inv, merge, lift))
-
-    base = targets - ridge[0] * coefs
-    base_rows = lax.dynamic_update_slice(
-        jnp.zeros((leaf_size, target_width), jnp.float32), base, (col_pos * share_rows, 0)
+                whole = jnp.concatenate(exchange(whole, "leaf", leaf_pos, digit_low, fan), axis=0)
+            lift = mm(own_inv, whole)
+        shared.append((node_inv, own_inv, transfer, lift))
+
+    blocks = list(
+        band_products(rows_x, fetched, targets, ridge, tile_mask, col_pos, col_count)
     )
-    groups = [[0]]
-    for reach in range(1, band_reach + 1):
-        groups.append([-reach, reach])
-    partial = base_rows
-    for group in groups:
-        kernel = jnp.concatenate([kernel_of(offset) for offset in group], axis=1)
-        group_coefs = jnp.concatenate([fetched[offset][:, features:] for offset in group], axis=0)
-        partial = partial - mm(kernel, group_coefs)
-    bit = 0
-    pieces = partial.reshape(leaf_size, target_width)
-    while 1 << bit < col_count:
-        width = col_width << bit
-        view = pieces.reshape(leaf_size, -1, 2, col_width)
-        side = (col_pos >> bit) % 2
-        keep = lax.dynamic_slice_in_dim(view, side, 1, 2).reshape(leaf_size, -1)
-        give = lax.dynamic_slice_in_dim(view, 1 - side, 1, 2).reshape(leaf_size, -1)
-        pieces = keep + partner_of(give, "col", 1 << bit)
-        bit += 1
-    residual = pieces
+    ready = blocks[-1]
+    mask = 1
+    while mask < col_count:
+        for m in range(col_count - 2 * mask, -1, -2 * mask):
+            blocks[m] = blocks[m] + partner_of(blocks[m + mask], "col", mask)
+        mask *= 2
+    residual = blocks[0]
+    late_solve, late_basis, _ = lax.optimization_barrier((solve, basis, ready))
+    down_map = mm_t(spread, mm(late_solve, late_basis))
 
     current = mm(up_map, residual)
     stacks = []
@@ -198,12 +258,14 @@
         stacked = jnp.concatenate(ordered, axis=0)
         stacks.append(stacked)
         if number < len(levels) - 1:
-            current = mm(shared[number][1], stacked)
+            current = mm_t(shared[number][2], mm(shared[number][0], stacked))
+            for fan, digit_low in [level[:2] for level in levels[: number + 1]]:
+                current = sum(exchange_raw(current, "leaf", digit_low, fan))
     values = None
     for number in range(len(levels) - 1, -1, -1):
-        own_inv, merge, lift = shared[number]
+        node_inv, own_inv, transfer, lift = shared[number]
         fresh_values = mm(own_inv, stacks[number])
-        values = fresh_values if values is None else fresh_values - mm_t(lift, values)
+        values = fresh_values if values is None else fresh_values - mm(lift, values)
     children = levels[0][0]
     local_index = leaf_pos % children
     raw = exchange_raw(values, "leaf", 0, children)

time: 200 us -> 126 us (0.63)
  matrix products: 43.8 us -> 19.8 us
  blocking collectives: 26.9 us -> 7.2 us
  local copies, waits for them, and re-layouts: 22.9 us -> 4.7 us
  between operations: 28.2 us -> 10.9 us
  other arithmetic: 19 us -> 2.7 us
  Pallas kernels: 0 us -> 12.6 us
  waiting for transfers between devices: 20.5 us -> 28.1 us
  starting transfers between devices: 37.3 us -> 39.9 us
    all_gather x1 -> x0, blocking collectives: 19.5 us -> none  [local(): every = lax.all_gather(mine, 'col', axis=1, tiled=True)]
    dot_general x13 -> x10, matrix products: 26.3 us -> 10.7 us  [mm(): return jnp.dot(a, b, precision=high)]
    pallas_call x0 -> x1, Pallas kernels: none -> 12.6 us  [band_products(): pl.pallas_call(functools.partial(band_body, count, features, cols), grid=...]
    ppermute x23 -> x25, waiting for transfers between devices: 20.5 us -> 28.1 us  [partner_of(): return lax.ppermute(block, axis, swap_route(lax.axis_size(axis), mask))]
    dot_general x6 -> x0, matrix products: 6.72 us -> none  [the longest x5 6.15 us: kernel_of(): inner = jnp.einsum('pf,qf->pq', rows_x, column_points, precision=high)]
    dynamic_slice x5 -> x0, local copies, waits for them, and re-layouts: 6.07 us -> none  [the longest x3 4.42 us: local(): keep = lax.dynamic_slice_in_dim(view, side, 1, 2).reshape(leaf_size, -1)]
    ppermute x23 -> x25, starting transfers between devices: 23 us -> 29 us  [partner_of(): return lax.ppermute(block, axis, swap_route(lax.axis_size(axis), mask))]
    reduce_sum x6 -> x0, other arithmetic: 5.08 us -> none  [the longest x5 4.88 us: kernel_of(): squares = jnp.sum(column_points * column_points, axis=1)]
  transfers between devices with their start and end apart: 28 -> 29, of which waited for: 9 -> 13; matrix products, arithmetic and copies ran while one was open for 39% -> 19% of each run, Pallas kernels for 0% -> 10%
where the time goes in v2:
time: 126 us
  starting transfers between devices  39.9 us (32%)
  waiting for transfers between devices  28.1 us (22%)
  matrix products  19.8 us (16%)
  Pallas kernels  12.6 us (10%)
  between operations  10.9 us (9%)
  blocking collectives  7.2 us (6%)
  local copies, waits for them, and re-layouts  4.7 us (4%)
  other arithmetic  2.7 us (2%)
    ppermute x25, starting transfers between devices, partner_of(): return lax.ppermute(block, axis, swap_route(lax.axis_size(axis), mask))  29 us
    ppermute x25, waiting for transfers between devices, partner_of(): return lax.ppermute(block, axis, swap_route(lax.axis_size(axis), mask))  28.1 us
    pallas_call x1, Pallas kernels, band_products(): pl.pallas_call(functools.partial(band_body, count, features, cols), grid=...  12.6 us
    ppermute x4, starting transfers between devices, shifted(): lax.ppermute(value, axis, [(source, source + steps) for source in range(i...  11 us
    dot_general x10, matrix products, mm(): return jnp.dot(a, b, precision=high)  10.7 us
    dot_general x4, matrix products, mm_t(): return jnp.einsum('ka,kc->ac', a, b, precision=high)  9.07 us
    all_gather x1, blocking collectives, local(): rows_x = lax.all_gather(points, 'col', axis=0, tiled=True)  7.2 us
  transfers between devices with their start and end apart: 29, of which 13 were waited for; matrix products, arithmetic and copies ran while one was open for 19% of the time, Pallas kernels for 10%

profile of v2, /device:TPU:0, one launch (start us, length us, event | category | flops | bytes accessed | tf_op | source)
XLA Modules:
  0.0 125.9 jit_solution(13603112320397055262)
XLA Ops:
  2.8 5.0 %collective-permute-start = (f32[256,640]{1,0:T(8,128)S(1)}, f32[256,640]{1,0:T(8,128)S(1)}, u32[]{:S(2)}, u32[]{:S(2)}) collective-permute-start(f32[256,640]{1,0:T(8,128)S(1)} %constant_dynamic-update-slice_fusion.refs_7_), channel_id=1, source_target_pairs={{0,8},{4,12},{8,16},{12,20},{16,24},{20,28},{1,9},{5,13},{9,17},{1... | collective-permute-start | bytes 1966088 | tf_op jit(solution)/shard_map/ppermute | solution.py:24
  7.8 3.4 %collective-permute-start.1 = (f32[256,640]{1,0:T(8,128)S(1)}, f32[256,640]{1,0:T(8,128)S(1)}, u32[]{:S(2)}, u32[]{:S(2)}) collective-permute-start(f32[256,640]{1,0:T(8,128)S(1)} %constant_dynamic-update-slice_fusion.refs_7_), channel_id=1, source_target_pairs={{0,4},{4,8},{8,12},{12,16},{16,20},{20,24},{24,28},{1,5},{5,9},{9,... | collective-permute-start | bytes 1966088 | tf_op jit(solution)/shard_map/ppermute | solution.py:24
  11.2 1.3 %collective-permute-start.2 = (f32[256,640]{1,0:T(8,128)S(1)}, f32[256,640]{1,0:T(8,128)}, u32[]{:S(2)}, u32[]{:S(2)}) collective-permute-start(f32[256,640]{1,0:T(8,128)S(1)} %constant_dynamic-update-slice_fusion.refs_7_), channel_id=1, source_target_pairs={{4,0},{8,4},{12,8},{16,12},{20,16},{24,20},{28,24},{5,1},{9,5},{13... | collective-permute-start | bytes 1966088 | tf_op jit(solution)/shard_map/ppermute | solution.py:24
  12.5 1.3 %collective-permute-start.3 = (f32[256,640]{1,0:T(8,128)S(1)}, f32[256,640]{1,0:T(8,128)}, u32[]{:S(2)}, u32[]{:S(2)}) collective-permute-start(f32[256,640]{1,0:T(8,128)S(1)} %constant_dynamic-update-slice_fusion.refs_7_), channel_id=1, source_target_pairs={{8,0},{12,4},{16,8},{20,12},{24,16},{28,20},{9,1},{13,5},{17,9},{2... | collective-permute-start | bytes 1966088 | tf_op jit(solution)/shard_map/ppermute | solution.py:24
  13.8 1.6 %slice_bitcast_fusion.1 = f32[64,512]{1,0:T(8,128)} fusion(f32[1,320,1024]{2,1,0:T(8,128)} %param.20), kind=kLoop, calls=%fused_computation.51 | loop fusion | bytes 262144 | tf_op jit(solution)/shard_map/squeeze | solution.py:217
  15.4 4.7 %collective-permute-start.16 = (f32[64,512]{1,0:T(8,128)}, f32[64,512]{1,0:T(8,128)S(1)}, u32[]{:S(2)}, u32[]{:S(2)}) collective-permute-start(f32[64,512]{1,0:T(8,128)} %slice_bitcast_fusion.1), channel_id=1, source_target_pairs={{0,12},{4,8},{8,4},{12,0},{16,28},{20,24},{24,20},{28,16},{1,13},{... | collective-permute-start | bytes 393224 | tf_op jit(solution)/shard_map/ppermute | solution.py:18
  20.1 1.4 %fusion.47 = (s32[]{:T(128)}, s32[4]{0:T(128)S(1)}) fusion(s32[]{:T(128)S(6)} %select_n.302, s32[]{:T(128)S(6)} %mul.46, s32[8]{0:T(128)} %param.17, s32[]{:T(128)S(6)} %select_n.301), kind=kLoop, calls=%fused_computation.101 | loop fusion | flops 15 | bytes 48 | tf_op jit(solution)/shard_map/reduce_sum | solution.py:272
  31.9 4.2 %fusion.51 = f32[256,1024]{1,0:T(8,128)S(1)} fusion(f32[1,1024,256]{2,1,0:T(8,128)S(1)} %copy-done, f32[1,1024,1024]{2,1,0:T(8,128)} %param.18), kind=kOutput, calls=%fused_computation.106 | convolution fusion | flops 1610612736 | bytes 6291456 | tf_op jit(solution)/shard_map/ka,kc->ac/dot_general | solution.py:65
  36.1 1.7 %fusion = f32[256,1024]{1,0:T(8,128)S(1)} fusion(f32[256,1024]{1,0:T(8,128)S(1)} %fusion.51, s32[1024]{0:T(1024)S(1)} %bitcast.67), kind=kOutput, calls=%fused_computation.1 | convolution fusion | flops 1611661312 | bytes 2101248 | tf_op jit(solution)/shard_map/dot_general | solution.py:61
  37.8 7.2 %all_gather.3.refs_3_ = f32[1024,128]{1,0:T(8,128)S(1)} all-gather(f32[256,128]{1,0:T(8,128)S(1)} %copy-done.7), channel_id=1, replica_groups=mesh['leaf'=8,'col'=4] {'col'}, dimensions={0}, use_global_device_ids=true | all-gather | bytes 655360 | tf_op jit(solution)/shard_map/all_gather | solution.py:204
  45.1 4.7 %collective-permute-start.14 = (f32[256,256]{1,0:T(8,128)S(1)}, f32[256,256]{1,0:T(8,128)S(1)}, u32[]{:S(2)}, u32[]{:S(2)}) collective-permute-start(f32[256,256]{1,0:T(8,128)S(1)} %slice_bitcast_fusion), channel_id=1, source_target_pairs={{0,8},{4,12},{8,0},{12,4},{16,24},{20,28},{24,16},{28,20},{1,9},{5... | collective-permute-start | bytes 786440 | tf_op jit(solution)/shard_map/ppermute | solution.py:18
  50.3 1.5 %collective-permute-start.18 = (f32[64,512]{1,0:T(8,128)}, f32[64,512]{1,0:T(8,128)S(1)}, u32[]{:S(2)}, u32[]{:S(2)}) collective-permute-start(f32[64,512]{1,0:T(8,128)} %slice_bitcast_fusion.1), channel_id=1, source_target_pairs={{0,4},{4,0},{8,12},{12,8},{16,20},{20,16},{24,28},{28,24},{1,5},{5... | collective-permute-start | bytes 393224 | tf_op jit(solution)/shard_map/ppermute | solution.py:18
  51.9 12.6 %shard_map.122 = (f32[1024,128]{1,0:T(8,128)S(1)}, f32[1024,128]{1,0:T(8,128)S(1)}, f32[1024,128]{1,0:T(8,128)S(1)}, f32[1024,128]{1,0:T(8,128)S(1)}) custom-call(s32[1,5]{1,0:T(1,128)S(1)} %copy-done.2, f32[1]{0:T(128)S(6)} %copy.24.refs_1_, s32[1]{0:T(128)} %bitcast.refs_2_, f32[1024,128]{1,0:T(8,128)S(1)} %all_gather.3.refs_3_, f32[256,512]{1,0:T(8,128)S(1)} %copy-done.1, ...), custom_call_target="tpu_custom_call" | custom-call | flops 5033164800 | bytes 4194304 | tf_op jit(solution)/shard_map/pallas_call | solution.py:153
  66.5 1.5 %collective-permute-start.6 = (f32[1024,128]{1,0:T(8,128)S(1)}, f32[1024,128]{1,0:T(8,128)S(1)}, u32[]{:S(2)}, u32[]{:S(2)}) collective-permute-start(f32[1024,128]{1,0:T(8,128)S(1)} %add.83), channel_id=1, source_target_pairs={{0,2},{1,3},{2,0},{3,1},{4,6},{5,7},{6,4},{7,5},{8,10},{9,11},{10,... | collective-permute-start | bytes 1572872 | tf_op jit(solution)/shard_map/ppermute | solution.py:18
  69.1 1.8 %fusion.57 = f32[1024,256]{1,0:T(8,128)S(1)} fusion(f32[1024,1024]{1,0:T(8,128)S(1)} %bitcast.66, f32[1024,256]{1,0:T(8,128)S(1)} %bitcast.65), kind=kOutput, calls=%fused_computation.112 | convolution fusion | flops 1610612736 | bytes 6291456 | tf_op jit(solution)/shard_map/dot_general | solution.py:61
  70.9 9.6 %collective-permute-done.6 = f32[1024,128]{1,0:T(8,128)S(1)} collective-permute-done((f32[1024,128]{1,0:T(8,128)S(1)}, f32[1024,128]{1,0:T(8,128)S(1)}, u32[]{:S(2)}, u32[]{:S(2)}) %collective-permute-start.6) | collective-permute-done | bytes 524320 | tf_op jit(solution)/shard_map/ppermute | solution.py:18
  81.8 2.9 %collective-permute-start.12 = (f32[256,128]{1,0:T(8,128)S(1)}, f32[256,128]{1,0:T(8,128)S(1)}, u32[]{:S(2)}, u32[]{:S(2)}) collective-permute-start(f32[256,128]{1,0:T(8,128)S(1)} %fusion.58), channel_id=1, source_target_pairs={{0,12},{4,8},{8,4},{12,0},{16,28},{20,24},{24,20},{28,16},{1,13},{... | collective-permute-start | bytes 393224 | tf_op jit(solution)/shard_map/ppermute | solution.py:18
  84.8 2.5 %fusion.1 = f32[1024,256]{1,0:T(8,128)S(1)} fusion(f32[1024,256]{1,0:T(8,128)S(1)} %fusion.57, s32[1024]{0:T(1024)S(1)} %bitcast.68), kind=kOutput, calls=%fused_computation.2 | convolution fusion | flops 1611661312 | bytes 2101248 | tf_op jit(solution)/shard_map/ka,kc->ac/dot_general | solution.py:65
  87.5 1.5 %collective-permute-start.8 = (f32[256,128]{1,0:T(8,128)S(1)}, f32[256,128]{1,0:T(8,128)S(1)}, u32[]{:S(2)}, u32[]{:S(2)}) collective-permute-start(f32[256,128]{1,0:T(8,128)S(1)} %get-tuple-element.37), channel_id=1, source_target_pairs={{0,2},{1,3},{2,0},{3,1},{4,6},{5,7},{6,4},{7,5},{8,10},{9,11},{10,... | collective-permute-start | bytes 393224 | tf_op jit(solution)/shard_map/ppermute | solution.py:18
  91.2 1.6 %collective-permute-start.21 = (f32[256,128]{0,1:T(8,128)S(1)}, f32[256,128]{0,1:T(8,128)S(1)}, u32[]{:S(2)}, u32[]{:S(2)}) collective-permute-start(f32[256,128]{0,1:T(8,128)S(1)} %convolution_bitcast_fusion), channel_id=1, source_target_pairs={{0,12},{4,8},{8,4},{12,0},{16,28},{20,24},{24,20},{28,16},{1,13},{... | collective-permute-start | bytes 393224 | tf_op jit(solution)/shard_map/ppermute | solution.py:18
  93.3 1.5 %collective-permute-start.19 = (f32[256,128]{0,1:T(8,128)S(1)}, f32[256,128]{0,1:T(8,128)S(1)}, u32[]{:S(2)}, u32[]{:S(2)}) collective-permute-start(f32[256,128]{0,1:T(8,128)S(1)} %convolution_bitcast_fusion), channel_id=1, source_target_pairs={{0,4},{4,0},{8,12},{12,8},{16,20},{20,16},{24,28},{28,24},{1,5},{5... | collective-permute-start | bytes 393224 | tf_op jit(solution)/shard_map/ppermute | solution.py:18
  94.8 1.3 %fusion.3 = f32[1024,128]{1,0:T(8,128)S(1)} fusion(f32[1024,128]{1,0:T(8,128)S(1)} %add_add_fusion, s32[1024]{0:T(1024)S(1)} %bitcast.69), kind=kOutput, calls=%fused_computation.4 | convolution fusion | flops 806354944 | bytes 1052672 | tf_op jit(solution)/shard_map/dot_general | solution.py:61
  96.1 2.2 %collective-permute-done.21 = f32[256,128]{0,1:T(8,128)S(1)} collective-permute-done((f32[256,128]{0,1:T(8,128)S(1)}, f32[256,128]{0,1:T(8,128)S(1)}, u32[]{:S(2)}, u32[]{:S(2)}) %collective-permute-start.21) | collective-permute-done | bytes 131104 | tf_op jit(solution)/shard_map/ppermute | solution.py:18
  99.4 1.5 %collective-permute-start.22 = (f32[256,128]{0,1:T(8,128)S(1)}, f32[256,128]{0,1:T(8,128)S(1)}, u32[]{:S(2)}, u32[]{:S(2)}) collective-permute-start(f32[256,128]{0,1:T(8,128)S(1)} %add_add_fusion.1), channel_id=1, source_target_pairs={{0,16},{4,20},{8,24},{12,28},{16,0},{20,4},{24,8},{28,12},{1,17},{... | collective-permute-start | bytes 393224 | tf_op jit(solution)/shard_map/ppermute | solution.py:18
  100.9 2.4 %fusion.54 = f32[128,1024]{1,0:T(8,128)S(1)} fusion(f32[1024,128]{1,0:T(8,128)S(1)} %fusion.3, f32[1,1024,1024]{2,1,0:T(8,128)S(1)} %copy-done.3), kind=kOutput, calls=%fused_computation.109 | convolution fusion | flops 805306368 | bytes 5242880 | tf_op jit(solution)/shard_map/dot_general | solution.py:61
  103.3 4.5 %collective-permute-done.22 = f32[256,128]{0,1:T(8,128)S(1)} collective-permute-done((f32[256,128]{0,1:T(8,128)S(1)}, f32[256,128]{0,1:T(8,128)S(1)}, u32[]{:S(2)}, u32[]{:S(2)}) %collective-permute-start.22) | collective-permute-done | bytes 131104 | tf_op jit(solution)/shard_map/ppermute | solution.py:18
  108.6 2.0 %collective-permute-start.24 = (f32[256,128]{0,1:T(8,128)S(1)}, f32[256,128]{0,1:T(8,128)S(1)}, u32[]{:S(2)}, u32[]{:S(2)}) collective-permute-start(f32[256,128]{0,1:T(8,128)S(1)} %convolution_subtract_fusion.1), channel_id=1, source_target_pairs={{0,8},{4,12},{8,0},{12,4},{16,24},{20,28},{24,16},{28,20},{1,9},{5... | collective-permute-start | bytes 393224 | tf_op jit(solution)/shard_map/ppermute | solution.py:18
  110.6 1.5 %collective-permute-start.25 = (f32[256,128]{0,1:T(8,128)S(1)}, f32[256,128]{0,1:T(8,128)S(1)}, u32[]{:S(2)}, u32[]{:S(2)}) collective-permute-start(f32[256,128]{0,1:T(8,128)S(1)} %convolution_subtract_fusion.1), channel_id=1, source_target_pairs={{0,4},{4,0},{8,12},{12,8},{16,20},{20,16},{24,28},{28,24},{1,5},{5... | collective-permute-start | bytes 393224 | tf_op jit(solution)/shard_map/ppermute | solution.py:18
  112.1 2.1 %fusion.4 = f32[1024,128]{1,0:T(8,128)S(1)} fusion(f32[128,1024]{1,0:T(8,128)S(1)} %fusion.54, s32[1024]{0:T(1024)S(1)} %bitcast.70), kind=kOutput, calls=%fused_computation.5 | convolution fusion | flops 807403520 | bytes 1052672 | tf_op jit(solution)/shard_map/ka,kc->ac/dot_general | solution.py:65
  117.3 1.3 %collective-permute-done.9 = f32[256,128]{1,0:T(8,128)S(1)} collective-permute-done((f32[256,128]{1,0:T(8,128)S(1)}, f32[256,128]{1,0:T(8,128)S(1)}, u32[]{:S(2)}, u32[]{:S(2)}) %collective-permute-start.9) | collective-permute-done | bytes 131104 | tf_op jit(solution)/shard_map/ppermute | solution.py:18
  119.5 3.5 %collective-permute-done.27 = f32[256,128]{1,0:T(8,128)S(1)} collective-permute-done((f32[256,128]{1,0:T(8,128)S(1)}, f32[256,128]{1,0:T(8,128)S(1)}, u32[]{:S(2)}, u32[]{:S(2)}) %collective-permute-start.27) | collective-permute-done | bytes 131104 | tf_op jit(solution)/shard_map/ppermute | solution.py:18
  123.0 2.0 %collective-permute-done.28 = f32[256,128]{1,0:T(8,128)S(1)} collective-permute-done((f32[256,128]{1,0:T(8,128)S(1)}, f32[256,128]{1,0:T(8,128)S(1)}, u32[]{:S(2)}, u32[]{:S(2)}) %collective-permute-start.28) | collective-permute-done | bytes 131104 | tf_op jit(solution)/shard_map/ppermute | solution.py:18
  (87 shorter events, 17.2 us)
Async XLA Ops:
  0.6 31.2 %copy-start = (f32[1,1024,256]{2,1,0:T(8,128)S(1)}, f32[1,1024,256]{2,1,0:T(8,128)}, u32[]{:S(2)}) copy-start(f32[1,1024,256]{2,1,0:T(8,128)} %param.19) | copy-start | bytes 3145732
  0.6 35.4 %copy-start.5 = (f32[1,320,256]{2,1,0:T(8,128)S(1)}, f32[1,320,256]{2,1,0:T(8,128)}, u32[]{:S(2)}) copy-start(f32[1,320,256]{2,1,0:T(8,128)} %param.21) | copy-start | bytes 983044
  1.7 34.4 %copy-start.9 = (s32[1,1024]{1,0:T(1,128)S(1)}, s32[1,1024]{1,0:T(1,128)}, u32[]{:S(2)}) copy-start(s32[1,1024]{1,0:T(1,128)} %param.16) | copy-start | bytes 12292
  2.8 42.3 %collective-permute-start = (f32[256,640]{1,0:T(8,128)S(1)}, f32[256,640]{1,0:T(8,128)S(1)}, u32[]{:S(2)}, u32[]{:S(2)}) collective-permute-start(f32[256,640]{1,0:T(8,128)S(1)} %constant_dynamic-update-slice_fusion.refs_7_), channel_id=1, source_target_pairs={{0,8},{4,12},{8,16},{12,20},{16,24},{20,28},{1,9},{5,13},{9,17},{1... | collective-permute-start | bytes 1966088 | tf_op jit(solution)/shard_map/ppermute | solution.py:24
  7.8 42.0 %collective-permute-start.1 = (f32[256,640]{1,0:T(8,128)S(1)}, f32[256,640]{1,0:T(8,128)S(1)}, u32[]{:S(2)}, u32[]{:S(2)}) collective-permute-start(f32[256,640]{1,0:T(8,128)S(1)} %constant_dynamic-update-slice_fusion.refs_7_), channel_id=1, source_target_pairs={{0,4},{4,8},{8,12},{12,16},{16,20},{20,24},{24,28},{1,5},{5,9},{9,... | collective-permute-start | bytes 1966088 | tf_op jit(solution)/shard_map/ppermute | solution.py:24
  11.2 38.6 %collective-permute-start.2 = (f32[256,640]{1,0:T(8,128)S(1)}, f32[256,640]{1,0:T(8,128)}, u32[]{:S(2)}, u32[]{:S(2)}) collective-permute-start(f32[256,640]{1,0:T(8,128)S(1)} %constant_dynamic-update-slice_fusion.refs_7_), channel_id=1, source_target_pairs={{4,0},{8,4},{12,8},{16,12},{20,16},{24,20},{28,24},{5,1},{9,5},{13... | collective-permute-start | bytes 1966088 | tf_op jit(solution)/shard_map/ppermute | solution.py:24
  12.5 37.8 %collective-permute-start.3 = (f32[256,640]{1,0:T(8,128)S(1)}, f32[256,640]{1,0:T(8,128)}, u32[]{:S(2)}, u32[]{:S(2)}) collective-permute-start(f32[256,640]{1,0:T(8,128)S(1)} %constant_dynamic-update-slice_fusion.refs_7_), channel_id=1, source_target_pairs={{8,0},{12,4},{16,8},{20,12},{24,16},{28,20},{9,1},{13,5},{17,9},{2... | collective-permute-start | bytes 1966088 | tf_op jit(solution)/shard_map/ppermute | solution.py:24
  15.4 29.7 %collective-permute-start.16 = (f32[64,512]{1,0:T(8,128)}, f32[64,512]{1,0:T(8,128)S(1)}, u32[]{:S(2)}, u32[]{:S(2)}) collective-permute-start(f32[64,512]{1,0:T(8,128)} %slice_bitcast_fusion.1), channel_id=1, source_target_pairs={{0,12},{4,8},{8,4},{12,0},{16,28},{20,24},{24,20},{28,16},{1,13},{... | collective-permute-start | bytes 393224 | tf_op jit(solution)/shard_map/ppermute | solution.py:18
  45.0 19.6 %collective-permute-start.13 = (f32[256,256]{1,0:T(8,128)S(1)}, f32[256,256]{1,0:T(8,128)S(1)}, u32[]{:S(2)}, u32[]{:S(2)}) collective-permute-start(f32[256,256]{1,0:T(8,128)S(1)} %slice_bitcast_fusion), channel_id=1, source_target_pairs={{0,12},{4,8},{8,4},{12,0},{16,28},{20,24},{24,20},{28,16},{1,13},{... | collective-permute-start | bytes 786440 | tf_op jit(solution)/shard_map/ppermute | solution.py:18
  45.1 19.6 %collective-permute-start.14 = (f32[256,256]{1,0:T(8,128)S(1)}, f32[256,256]{1,0:T(8,128)S(1)}, u32[]{:S(2)}, u32[]{:S(2)}) collective-permute-start(f32[256,256]{1,0:T(8,128)S(1)} %slice_bitcast_fusion), channel_id=1, source_target_pairs={{0,8},{4,12},{8,0},{12,4},{16,24},{20,28},{24,16},{28,20},{1,9},{5... | collective-permute-start | bytes 786440 | tf_op jit(solution)/shard_map/ppermute | solution.py:18
  49.7 14.9 %collective-permute-start.15 = (f32[256,256]{1,0:T(8,128)S(1)}, f32[256,256]{1,0:T(8,128)S(1)}, u32[]{:S(2)}, u32[]{:S(2)}) collective-permute-start(f32[256,256]{1,0:T(8,128)S(1)} %slice_bitcast_fusion), channel_id=1, source_target_pairs={{0,4},{4,0},{8,12},{12,8},{16,20},{20,16},{24,28},{28,24},{1,5},{5... | collective-permute-start | bytes 786440 | tf_op jit(solution)/shard_map/ppermute | solution.py:18
  49.8 14.7 %collective-permute-start.17 = (f32[64,512]{1,0:T(8,128)}, f32[64,512]{1,0:T(8,128)S(1)}, u32[]{:S(2)}, u32[]{:S(2)}) collective-permute-start(f32[64,512]{1,0:T(8,128)} %slice_bitcast_fusion.1), channel_id=1, source_target_pairs={{0,8},{4,12},{8,0},{12,4},{16,24},{20,28},{24,16},{28,20},{1,9},{5... | collective-permute-start | bytes 393224 | tf_op jit(solution)/shard_map/ppermute | solution.py:18
  50.3 14.2 %collective-permute-start.18 = (f32[64,512]{1,0:T(8,128)}, f32[64,512]{1,0:T(8,128)S(1)}, u32[]{:S(2)}, u32[]{:S(2)}) collective-permute-start(f32[64,512]{1,0:T(8,128)} %slice_bitcast_fusion.1), channel_id=1, source_target_pairs={{0,4},{4,0},{8,12},{12,8},{16,20},{20,16},{24,28},{28,24},{1,5},{5... | collective-permute-start | bytes 393224 | tf_op jit(solution)/shard_map/ppermute | solution.py:18
  64.5 2.0 %collective-permute-start.5 = (f32[1024,128]{1,0:T(8,128)S(1)}, f32[1024,128]{1,0:T(8,128)S(1)}, u32[]{:S(2)}, u32[]{:S(2)}) collective-permute-start(f32[1024,128]{1,0:T(8,128)S(1)} %get-tuple-element.11), channel_id=1, source_target_pairs={{0,1},{1,0},{2,3},{3,2},{4,5},{5,4},{6,7},{7,6},{8,9},{9,8},{10,11... | collective-permute-start | bytes 1572872 | tf_op jit(solution)/shard_map/ppermute | solution.py:18
  64.8 6.1 %collective-permute-start.4 = (f32[1024,128]{1,0:T(8,128)S(1)}, f32[1024,128]{1,0:T(8,128)S(1)}, u32[]{:S(2)}, u32[]{:S(2)}) collective-permute-start(f32[1024,128]{1,0:T(8,128)S(1)} %get-tuple-element.9), channel_id=1, source_target_pairs={{0,1},{1,0},{2,3},{3,2},{4,5},{5,4},{6,7},{7,6},{8,9},{9,8},{10,11... | collective-permute-start | bytes 1572872 | tf_op jit(solution)/shard_map/ppermute | solution.py:18
  66.5 14.0 %collective-permute-start.6 = (f32[1024,128]{1,0:T(8,128)S(1)}, f32[1024,128]{1,0:T(8,128)S(1)}, u32[]{:S(2)}, u32[]{:S(2)}) collective-permute-start(f32[1024,128]{1,0:T(8,128)S(1)} %add.83), channel_id=1, source_target_pairs={{0,2},{1,3},{2,0},{3,1},{4,6},{5,7},{6,4},{7,5},{8,10},{9,11},{10,... | collective-permute-start | bytes 1572872 | tf_op jit(solution)/shard_map/ppermute | solution.py:18
  81.2 7.8 %collective-permute-start.10 = (f32[256,128]{1,0:T(8,128)S(1)}, f32[256,128]{1,0:T(8,128)S(1)}, u32[]{:S(2)}, u32[]{:S(2)}) collective-permute-start(f32[256,128]{1,0:T(8,128)S(1)} %fusion.58), channel_id=1, source_target_pairs={{0,4},{4,0},{8,12},{12,8},{16,20},{20,16},{24,28},{28,24},{1,5},{5... | collective-permute-start | bytes 393224 | tf_op jit(solution)/shard_map/ppermute | solution.py:18
  81.8 7.3 %collective-permute-start.12 = (f32[256,128]{1,0:T(8,128)S(1)}, f32[256,128]{1,0:T(8,128)S(1)}, u32[]{:S(2)}, u32[]{:S(2)}) collective-permute-start(f32[256,128]{1,0:T(8,128)S(1)} %fusion.58), channel_id=1, source_target_pairs={{0,12},{4,8},{8,4},{12,0},{16,28},{20,24},{24,20},{28,16},{1,13},{... | collective-permute-start | bytes 393224 | tf_op jit(solution)/shard_map/ppermute | solution.py:18
  84.7 5.6 %collective-permute-start.11 = (f32[256,128]{1,0:T(8,128)S(1)}, f32[256,128]{1,0:T(8,128)S(1)}, u32[]{:S(2)}, u32[]{:S(2)}) collective-permute-start(f32[256,128]{1,0:T(8,128)S(1)} %fusion.58), channel_id=1, source_target_pairs={{0,8},{4,12},{8,0},{12,4},{16,24},{20,28},{24,16},{28,20},{1,9},{5... | collective-permute-start | bytes 393224 | tf_op jit(solution)/shard_map/ppermute | solution.py:18
  87.4 26.8 %collective-permute-start.7 = (f32[256,128]{1,0:T(8,128)S(1)}, f32[256,128]{1,0:T(8,128)S(1)}, u32[]{:S(2)}, u32[]{:S(2)}) collective-permute-start(f32[256,128]{1,0:T(8,128)S(1)} %get-tuple-element.38), channel_id=1, source_target_pairs={{0,1},{1,0},{2,3},{3,2},{4,5},{5,4},{6,7},{7,6},{8,9},{9,8},{10,11... | collective-permute-start | bytes 393224 | tf_op jit(solution)/shard_map/ppermute | solution.py:18
  87.5 29.1 %collective-permute-start.8 = (f32[256,128]{1,0:T(8,128)S(1)}, f32[256,128]{1,0:T(8,128)S(1)}, u32[]{:S(2)}, u32[]{:S(2)}) collective-permute-start(f32[256,128]{1,0:T(8,128)S(1)} %get-tuple-element.37), channel_id=1, source_target_pairs={{0,2},{1,3},{2,0},{3,1},{4,6},{5,7},{6,4},{7,5},{8,10},{9,11},{10,... | collective-permute-start | bytes 393224 | tf_op jit(solution)/shard_map/ppermute | solution.py:18
  91.2 7.0 %collective-permute-start.21 = (f32[256,128]{0,1:T(8,128)S(1)}, f32[256,128]{0,1:T(8,128)S(1)}, u32[]{:S(2)}, u32[]{:S(2)}) collective-permute-start(f32[256,128]{0,1:T(8,128)S(1)} %convolution_bitcast_fusion), channel_id=1, source_target_pairs={{0,12},{4,8},{8,4},{12,0},{16,28},{20,24},{24,20},{28,16},{1,13},{... | collective-permute-start | bytes 393224 | tf_op jit(solution)/shard_map/ppermute | solution.py:18
  92.8 5.8 %collective-permute-start.20 = (f32[256,128]{0,1:T(8,128)S(1)}, f32[256,128]{0,1:T(8,128)S(1)}, u32[]{:S(2)}, u32[]{:S(2)}) collective-permute-start(f32[256,128]{0,1:T(8,128)S(1)} %convolution_bitcast_fusion), channel_id=1, source_target_pairs={{0,8},{4,12},{8,0},{12,4},{16,24},{20,28},{24,16},{28,20},{1,9},{5... | collective-permute-start | bytes 393224 | tf_op jit(solution)/shard_map/ppermute | solution.py:18
  93.3 6.1 %collective-permute-start.19 = (f32[256,128]{0,1:T(8,128)S(1)}, f32[256,128]{0,1:T(8,128)S(1)}, u32[]{:S(2)}, u32[]{:S(2)}) collective-permute-start(f32[256,128]{0,1:T(8,128)S(1)} %convolution_bitcast_fusion), channel_id=1, source_target_pairs={{0,4},{4,0},{8,12},{12,8},{16,20},{20,16},{24,28},{28,24},{1,5},{5... | collective-permute-start | bytes 393224 | tf_op jit(solution)/shard_map/ppermute | solution.py:18
  99.4 8.4 %collective-permute-start.22 = (f32[256,128]{0,1:T(8,128)S(1)}, f32[256,128]{0,1:T(8,128)S(1)}, u32[]{:S(2)}, u32[]{:S(2)}) collective-permute-start(f32[256,128]{0,1:T(8,128)S(1)} %add_add_fusion.1), channel_id=1, source_target_pairs={{0,16},{4,20},{8,24},{12,28},{16,0},{20,4},{24,8},{28,12},{1,17},{... | collective-permute-start | bytes 393224 | tf_op jit(solution)/shard_map/ppermute | solution.py:18
  108.5 6.0 %collective-permute-start.23 = (f32[256,128]{0,1:T(8,128)S(1)}, f32[256,128]{0,1:T(8,128)S(1)}, u32[]{:S(2)}, u32[]{:S(2)}) collective-permute-start(f32[256,128]{0,1:T(8,128)S(1)} %convolution_subtract_fusion.1), channel_id=1, source_target_pairs={{0,12},{4,8},{8,4},{12,0},{16,28},{20,24},{24,20},{28,16},{1,13},{... | collective-permute-start | bytes 393224 | tf_op jit(solution)/shard_map/ppermute | solution.py:18
  108.6 6.3 %collective-permute-start.24 = (f32[256,128]{0,1:T(8,128)S(1)}, f32[256,128]{0,1:T(8,128)S(1)}, u32[]{:S(2)}, u32[]{:S(2)}) collective-permute-start(f32[256,128]{0,1:T(8,128)S(1)} %convolution_subtract_fusion.1), channel_id=1, source_target_pairs={{0,8},{4,12},{8,0},{12,4},{16,24},{20,28},{24,16},{28,20},{1,9},{5... | collective-permute-start | bytes 393224 | tf_op jit(solution)/shard_map/ppermute | solution.py:18
  110.6 5.3 %collective-permute-start.25 = (f32[256,128]{0,1:T(8,128)S(1)}, f32[256,128]{0,1:T(8,128)S(1)}, u32[]{:S(2)}, u32[]{:S(2)}) collective-permute-start(f32[256,128]{0,1:T(8,128)S(1)} %convolution_subtract_fusion.1), channel_id=1, source_target_pairs={{0,4},{4,0},{8,12},{12,8},{16,20},{20,16},{24,28},{28,24},{1,5},{5... | collective-permute-start | bytes 393224 | tf_op jit(solution)/shard_map/ppermute | solution.py:18
  114.2 4.5 %collective-permute-start.9 = (f32[256,128]{1,0:T(8,128)S(1)}, f32[256,128]{1,0:T(8,128)S(1)}, u32[]{:S(2)}, u32[]{:S(2)}) collective-permute-start(f32[256,128]{1,0:T(8,128)S(1)} %get-tuple-element.36), channel_id=1, source_target_pairs={{0,3},{1,2},{2,1},{3,0},{4,7},{5,6},{6,5},{7,4},{8,11},{9,10},{10,... | collective-permute-start | bytes 393224 | tf_op jit(solution)/shard_map/ppermute | solution.py:18
  116.6 3.0 %collective-permute-start.26 = (f32[256,128]{1,0:T(8,128)S(1)}, f32[256,128]{1,0:T(8,128)S(1)}, u32[]{:S(2)}, u32[]{:S(2)}) collective-permute-start(f32[256,128]{1,0:T(8,128)S(1)} %get-tuple-element.31), channel_id=1, source_target_pairs={{0,1},{1,0},{2,3},{3,2},{4,5},{5,4},{6,7},{7,6},{8,9},{9,8},{10,11... | collective-permute-start | bytes 393224 | tf_op jit(solution)/shard_map/ppermute | solution.py:18
  116.7 6.4 %collective-permute-start.27 = (f32[256,128]{1,0:T(8,128)S(1)}, f32[256,128]{1,0:T(8,128)S(1)}, u32[]{:S(2)}, u32[]{:S(2)}) collective-permute-start(f32[256,128]{1,0:T(8,128)S(1)} %get-tuple-element.30), channel_id=1, source_target_pairs={{0,2},{1,3},{2,0},{3,1},{4,6},{5,7},{6,4},{7,5},{8,10},{9,11},{10,... | collective-permute-start | bytes 393224 | tf_op jit(solution)/shard_map/ppermute | solution.py:18
  118.7 6.3 %collective-permute-start.28 = (f32[256,128]{1,0:T(8,128)S(1)}, f32[256,128]{1,0:T(8,128)S(1)}, u32[]{:S(2)}, u32[]{:S(2)}) collective-permute-start(f32[256,128]{1,0:T(8,128)S(1)} %get-tuple-element.29), channel_id=1, source_target_pairs={{0,3},{1,2},{2,1},{3,0},{4,7},{5,6},{6,5},{7,4},{8,11},{9,10},{10,... | collective-permute-start | bytes 393224 | tf_op jit(solution)/shard_map/ppermute | solution.py:18
  (7 other events, 87.3 us)

commit v3 on v2

--- a/solution.py
+++ b/solution.py
@@ -201,7 +201,7 @@
     fetched = []
     for offset in range(-band_reach, band_reach + 1):
         fetched.append(shifted(packed, "leaf", -offset) if offset else packed)
-    rows_x = lax.all_gather(points, "col", axis=0, tiled=True)
+    rows_x = jnp.concatenate(exchange(points, "col", col_pos, 0, col_count), axis=0)
 
     basis = leaf_basis[0]
     solve = leaf_inverse[0]

time: 126 us -> 138 us (1.095)
  starting transfers between devices: 39.9 us -> 54.7 us
  blocking collectives: 7.2 us -> 0 us
  matrix products: 19.8 us -> 22.9 us
  other arithmetic: 2.7 us -> 5.12 us
  waiting for transfers between devices: 28.1 us -> 26.5 us
    ppermute x25 -> x28, starting transfers between devices: 29 us -> 47.5 us  [partner_of(): return lax.ppermute(block, axis, swap_route(lax.axis_size(axis), mask))]
    all_gather x1 -> x0, blocking collectives: 7.2 us -> none  [local(): rows_x = lax.all_gather(points, 'col', axis=0, tiled=True)]
    ppermute x25 -> x28, waiting for transfers between devices: 28.1 us -> 24.2 us  [partner_of(): return lax.ppermute(block, axis, swap_route(lax.axis_size(axis), mask))]
    ppermute x4, starting transfers between devices: 11 us -> 7.23 us  [shifted(): lax.ppermute(value, axis, [(source, source + steps) for source in range(i...]
    ppermute x4, waiting for transfers between devices: 0.01 us -> 2.29 us  [shifted(): lax.ppermute(value, axis, [(source, source + steps) for source in range(i...]
    dot_general x10, matrix products: 10.7 us -> 12.9 us  [mm(): return jnp.dot(a, b, precision=high)]
    select_n x3 -> x4, other arithmetic: 0.19 us -> 2.06 us  [in_order(): jnp.where(odd, pieces[m ^ 1 << bit], pieces[m])]
    squeeze x1, local copies, waits for them, and re-layouts: 0.02 us -> 1.67 us  [local(): transfer = node_transfer[0, offset:offset + slice_count]]
  transfers between devices with their start and end apart: 29 -> 32, of which waited for: 13 -> 14; matrix products, arithmetic and copies ran while one was open for 19% -> 22% of each run, Pallas kernels for 10% -> 9%
where the time goes in v3:
time: 138 us; the launch traced here: 137 us
  starting transfers between devices  54.7 us (40%)
  waiting for transfers between devices  26.5 us (19%)
  matrix products  22.9 us (17%)
  Pallas kernels  12.7 us (9%)
  between operations  10.8 us (8%)
  other arithmetic  5.12 us (4%)
  local copies, waits for them, and re-layouts  4.25 us (3%)
    ppermute x28, starting transfers between devices, partner_of(): return lax.ppermute(block, axis, swap_route(lax.axis_size(axis), mask))  47.5 us
    ppermute x28, waiting for transfers between devices, partner_of(): return lax.ppermute(block, axis, swap_route(lax.axis_size(axis), mask))  24.2 us
    dot_general x10, matrix products, mm(): return jnp.dot(a, b, precision=high)  12.9 us
    pallas_call x1, Pallas kernels, band_products(): pl.pallas_call(functools.partial(band_body, count, features, cols), grid=...  12.7 us
    dot_general x4, matrix products, mm_t(): return jnp.einsum('ka,kc->ac', a, b, precision=high)  10 us
    ppermute x4, starting transfers between devices, shifted(): lax.ppermute(value, axis, [(source, source + steps) for source in range(i...  7.23 us
  transfers between devices with their start and end apart: 32, of which 14 were waited for; matrix products, arithmetic and copies ran while one was open for 22% of the time, Pallas kernels for 9%

profile of v3, /device:TPU:0, one launch (start us, length us, event | category | flops | bytes accessed | tf_op | source)
XLA Modules:
  0.0 137.0 jit_solution(2439248470530639356)
XLA Ops:
  0.7 2.5 %collective-permute-start = (f32[256,128]{1,0:T(8,128)}, f32[256,128]{1,0:T(8,128)S(1)}, u32[]{:S(2)}, u32[]{:S(2)}) collective-permute-start(f32[256,128]{1,0:T(8,128)} %param.11), channel_id=1, source_target_pairs={{0,3},{1,2},{2,1},{3,0},{4,7},{5,6},{6,5},{7,4},{8,11},{9,10},{10,... | collective-permute-start | bytes 393224 | tf_op jit(solution)/shard_map/ppermute | solution.py:18
  3.8 1.5 %slice_bitcast_fusion.1 = f32[64,512]{1,0:T(8,128)} fusion(f32[1,320,1024]{2,1,0:T(8,128)} %param.20), kind=kLoop, calls=%fused_computation.52 | loop fusion | bytes 262144 | tf_op jit(solution)/shard_map/squeeze | solution.py:217
  5.4 2.7 %collective-permute-start.19 = (f32[64,512]{1,0:T(8,128)}, f32[64,512]{1,0:T(8,128)}, u32[]{:S(2)}, u32[]{:S(2)}) collective-permute-start(f32[64,512]{1,0:T(8,128)} %slice_bitcast_fusion.1), channel_id=1, source_target_pairs={{0,12},{4,8},{8,4},{12,0},{16,28},{20,24},{24,20},{28,16},{1,13},{... | collective-permute-start | bytes 393224 | tf_op jit(solution)/shard_map/ppermute | solution.py:18
  8.1 5.1 %fusion.51 = f32[256,1024]{1,0:T(8,128)} fusion(f32[1,1024,256]{2,1,0:T(8,128)S(1)} %copy-done, f32[1,1024,1024]{2,1,0:T(8,128)} %param.18), kind=kOutput, calls=%fused_computation.115 | convolution fusion | flops 1610612736 | bytes 6291456 | tf_op jit(solution)/shard_map/ka,kc->ac/dot_general | solution.py:65
  14.9 2.4 %collective-permute-start.3 = (f32[256,640]{1,0:T(8,128)S(1)}, f32[256,640]{1,0:T(8,128)S(1)}, u32[]{:S(2)}, u32[]{:S(2)}) collective-permute-start(f32[256,640]{1,0:T(8,128)S(1)} %constant_dynamic-update-slice_fusion.refs_7_), channel_id=1, source_target_pairs={{0,8},{4,12},{8,16},{12,20},{16,24},{20,28},{1,9},{5,13},{9,17},{1... | collective-permute-start | bytes 1966088 | tf_op jit(solution)/shard_map/ppermute | solution.py:24
  17.3 2.3 %collective-permute-start.4 = (f32[256,640]{1,0:T(8,128)S(1)}, f32[256,640]{1,0:T(8,128)S(1)}, u32[]{:S(2)}, u32[]{:S(2)}) collective-permute-start(f32[256,640]{1,0:T(8,128)S(1)} %constant_dynamic-update-slice_fusion.refs_7_), channel_id=1, source_target_pairs={{0,4},{4,8},{8,12},{12,16},{16,20},{20,24},{24,28},{1,5},{5,9},{9,... | collective-permute-start | bytes 1966088 | tf_op jit(solution)/shard_map/ppermute | solution.py:24
  22.8 1.7 %slice_bitcast_fusion = f32[256,256]{1,0:T(8,128)} fusion(f32[1,320,256]{2,1,0:T(8,128)} %param.21), kind=kLoop, calls=%fused_computation.46 | loop fusion | bytes 524288 | tf_op jit(solution)/shard_map/squeeze | solution.py:224
  24.5 3.9 %fusion = f32[256,1024]{1,0:T(8,128)} fusion(f32[256,1024]{1,0:T(8,128)} %fusion.51, s32[1024]{0:T(1024)S(1)} %bitcast.67), kind=kOutput, calls=%fused_computation.1 | convolution fusion | flops 1611661312 | bytes 2101248 | tf_op jit(solution)/shard_map/dot_general | solution.py:61
  39.2 6.6 %collective-permute-start.20 = (f32[64,512]{1,0:T(8,128)}, f32[64,512]{1,0:T(8,128)S(1)}, u32[]{:S(2)}, u32[]{:S(2)}) collective-permute-start(f32[64,512]{1,0:T(8,128)} %slice_bitcast_fusion.1), channel_id=1, source_target_pairs={{0,8},{4,12},{8,0},{12,4},{16,24},{20,28},{24,16},{28,20},{1,9},{5... | collective-permute-start | bytes 393224 | tf_op jit(solution)/shard_map/ppermute | solution.py:18
  46.4 2.3 %collective-permute-done.4.refs_6_ = f32[256,640]{1,0:T(8,128)S(1)} collective-permute-done((f32[256,640]{1,0:T(8,128)S(1)}, f32[256,640]{1,0:T(8,128)S(1)}, u32[]{:S(2)}, u32[]{:S(2)}) %collective-permute-start.4) | collective-permute-done | bytes 655392 | tf_op jit(solution)/shard_map/ppermute | solution.py:24
  48.7 4.8 %collective-permute-start.16 = (f32[256,256]{1,0:T(8,128)}, f32[256,256]{1,0:T(8,128)S(1)}, u32[]{:S(2)}, u32[]{:S(2)}) collective-permute-start(f32[256,256]{1,0:T(8,128)} %slice_bitcast_fusion), channel_id=1, source_target_pairs={{0,12},{4,8},{8,4},{12,0},{16,28},{20,24},{24,20},{28,16},{1,13},{... | collective-permute-start | bytes 786440 | tf_op jit(solution)/shard_map/ppermute | solution.py:18
  53.5 8.2 %collective-permute-start.17 = (f32[256,256]{1,0:T(8,128)}, f32[256,256]{1,0:T(8,128)S(1)}, u32[]{:S(2)}, u32[]{:S(2)}) collective-permute-start(f32[256,256]{1,0:T(8,128)} %slice_bitcast_fusion), channel_id=1, source_target_pairs={{0,8},{4,12},{8,0},{12,4},{16,24},{20,28},{24,16},{28,20},{1,9},{5... | collective-permute-start | bytes 786440 | tf_op jit(solution)/shard_map/ppermute | solution.py:18
  61.8 12.7 %shard_map.122 = (f32[1024,128]{1,0:T(8,128)S(1)}, f32[1024,128]{1,0:T(8,128)S(1)}, f32[1024,128]{1,0:T(8,128)S(1)}, f32[1024,128]{1,0:T(8,128)S(1)}) custom-call(s32[1,5]{1,0:T(1,128)S(1)} %copy-done.2, f32[1]{0:T(128)S(6)} %copy.24.refs_1_, s32[1]{0:T(128)} %bitcast.refs_2_, f32[1024,128]{1,0:T(8,128)S(1)} %pad_maximum_fusion.refs_3_, ...), custom_call_target="tpu_custom_call" | custom-call | flops 5033164800 | bytes 4194304 | tf_op jit(solution)/shard_map/pallas_call | solution.py:153
  76.5 1.6 %collective-permute-start.9 = (f32[1024,128]{1,0:T(8,128)S(1)}, f32[1024,128]{1,0:T(8,128)S(1)}, u32[]{:S(2)}, u32[]{:S(2)}) collective-permute-start(f32[1024,128]{1,0:T(8,128)S(1)} %add.95), channel_id=1, source_target_pairs={{0,2},{1,3},{2,0},{3,1},{4,6},{5,7},{6,4},{7,5},{8,10},{9,11},{10,... | collective-permute-start | bytes 1572872 | tf_op jit(solution)/shard_map/ppermute | solution.py:18
  79.2 1.9 %fusion.57 = f32[1024,256]{1,0:T(8,128)S(1)} fusion(f32[1024,1024]{1,0:T(8,128)S(1)} %bitcast.66, f32[1024,256]{1,0:T(8,128)S(1)} %bitcast.65), kind=kOutput, calls=%fused_computation.121 | convolution fusion | flops 1610612736 | bytes 6291456 | tf_op jit(solution)/shard_map/dot_general | solution.py:61
  81.1 9.5 %collective-permute-done.9 = f32[1024,128]{1,0:T(8,128)S(1)} collective-permute-done((f32[1024,128]{1,0:T(8,128)S(1)}, f32[1024,128]{1,0:T(8,128)S(1)}, u32[]{:S(2)}, u32[]{:S(2)}) %collective-permute-start.9) | collective-permute-done | bytes 524320 | tf_op jit(solution)/shard_map/ppermute | solution.py:18
  91.3 2.1 %collective-permute-start.13 = (f32[256,128]{1,0:T(8,128)S(1)}, f32[256,128]{1,0:T(8,128)S(1)}, u32[]{:S(2)}, u32[]{:S(2)}) collective-permute-start(f32[256,128]{1,0:T(8,128)S(1)} %fusion.58), channel_id=1, source_target_pairs={{0,4},{4,0},{8,12},{12,8},{16,20},{20,16},{24,28},{28,24},{1,5},{5... | collective-permute-start | bytes 393224 | tf_op jit(solution)/shard_map/ppermute | solution.py:18
  94.9 2.5 %fusion.1 = f32[1024,256]{1,0:T(8,128)S(1)} fusion(f32[1024,256]{1,0:T(8,128)S(1)} %fusion.57, s32[1024]{0:T(1024)S(1)} %bitcast.68), kind=kOutput, calls=%fused_computation.2 | convolution fusion | flops 1611661312 | bytes 2101248 | tf_op jit(solution)/shard_map/ka,kc->ac/dot_general | solution.py:65
  97.4 1.8 %collective-permute-done.14 = f32[256,128]{1,0:T(8,128)S(1)} collective-permute-done((f32[256,128]{1,0:T(8,128)S(1)}, f32[256,128]{1,0:T(8,128)S(1)}, u32[]{:S(2)}, u32[]{:S(2)}) %collective-permute-start.14) | collective-permute-done | bytes 131104 | tf_op jit(solution)/shard_map/ppermute | solution.py:18
  101.4 1.7 %collective-permute-start.22 = (f32[256,128]{0,1:T(8,128)S(1)}, f32[256,128]{0,1:T(8,128)S(1)}, u32[]{:S(2)}, u32[]{:S(2)}) collective-permute-start(f32[256,128]{0,1:T(8,128)S(1)} %convolution_bitcast_fusion), channel_id=1, source_target_pairs={{0,4},{4,0},{8,12},{12,8},{16,20},{20,16},{24,28},{28,24},{1,5},{5... | collective-permute-start | bytes 393224 | tf_op jit(solution)/shard_map/ppermute | solution.py:18
  109.3 1.7 %collective-permute-start.25 = (f32[256,128]{0,1:T(8,128)S(1)}, f32[256,128]{0,1:T(8,128)S(1)}, u32[]{:S(2)}, u32[]{:S(2)}) collective-permute-start(f32[256,128]{0,1:T(8,128)S(1)} %add_add_fusion.1), channel_id=1, source_target_pairs={{0,16},{4,20},{8,24},{12,28},{16,0},{20,4},{24,8},{28,12},{1,17},{... | collective-permute-start | bytes 393224 | tf_op jit(solution)/shard_map/ppermute | solution.py:18
  111.0 2.4 %fusion.54 = f32[128,1024]{1,0:T(8,128)S(1)} fusion(f32[1024,128]{1,0:T(8,128)S(1)} %fusion.3, f32[1,1024,1024]{2,1,0:T(8,128)S(1)} %copy-done.3), kind=kOutput, calls=%fused_computation.118 | convolution fusion | flops 805306368 | bytes 5242880 | tf_op jit(solution)/shard_map/dot_general | solution.py:61
  113.6 1.6 %collective-permute-done.25 = f32[256,128]{0,1:T(8,128)S(1)} collective-permute-done((f32[256,128]{0,1:T(8,128)S(1)}, f32[256,128]{0,1:T(8,128)S(1)}, u32[]{:S(2)}, u32[]{:S(2)}) %collective-permute-start.25) | collective-permute-done | bytes 131104 | tf_op jit(solution)/shard_map/ppermute | solution.py:18
  115.9 1.7 %collective-permute-start.26 = (f32[256,128]{0,1:T(8,128)S(1)}, f32[256,128]{0,1:T(8,128)S(1)}, u32[]{:S(2)}, u32[]{:S(2)}) collective-permute-start(f32[256,128]{0,1:T(8,128)S(1)} %convolution_subtract_fusion.1), channel_id=1, source_target_pairs={{0,12},{4,8},{8,4},{12,0},{16,28},{20,24},{24,20},{28,16},{1,13},{... | collective-permute-start | bytes 393224 | tf_op jit(solution)/shard_map/ppermute | solution.py:18
  117.6 2.8 %collective-permute-start.27 = (f32[256,128]{0,1:T(8,128)S(1)}, f32[256,128]{0,1:T(8,128)S(1)}, u32[]{:S(2)}, u32[]{:S(2)}) collective-permute-start(f32[256,128]{0,1:T(8,128)S(1)} %convolution_subtract_fusion.1), channel_id=1, source_target_pairs={{0,8},{4,12},{8,0},{12,4},{16,24},{20,28},{24,16},{28,20},{1,9},{5... | collective-permute-start | bytes 393224 | tf_op jit(solution)/shard_map/ppermute | solution.py:18
  120.4 2.1 %fusion.4 = f32[1024,128]{1,0:T(8,128)S(1)} fusion(f32[128,1024]{1,0:T(8,128)S(1)} %fusion.54, s32[1024]{0:T(1024)S(1)} %bitcast.70), kind=kOutput, calls=%fused_computation.5 | convolution fusion | flops 807403520 | bytes 1052672 | tf_op jit(solution)/shard_map/ka,kc->ac/dot_general | solution.py:65
  122.5 1.6 %collective-permute-start.11 = (f32[256,128]{1,0:T(8,128)S(1)}, f32[256,128]{1,0:T(8,128)S(1)}, u32[]{:S(2)}, u32[]{:S(2)}) collective-permute-start(f32[256,128]{1,0:T(8,128)S(1)} %get-tuple-element.37), channel_id=1, source_target_pairs={{0,2},{1,3},{2,0},{3,1},{4,6},{5,7},{6,4},{7,5},{8,10},{9,11},{10,... | collective-permute-start | bytes 393224 | tf_op jit(solution)/shard_map/ppermute | solution.py:18
  126.2 1.8 %collective-permute-done.11 = f32[256,128]{1,0:T(8,128)S(1)} collective-permute-done((f32[256,128]{1,0:T(8,128)S(1)}, f32[256,128]{1,0:T(8,128)S(1)}, u32[]{:S(2)}, u32[]{:S(2)}) %collective-permute-start.11) | collective-permute-done | bytes 131104 | tf_op jit(solution)/shard_map/ppermute | solution.py:18
  128.0 2.5 %collective-permute-start.30 = (f32[256,128]{1,0:T(8,128)S(1)}, f32[256,128]{1,0:T(8,128)S(1)}, u32[]{:S(2)}, u32[]{:S(2)}) collective-permute-start(f32[256,128]{1,0:T(8,128)S(1)} %get-tuple-element.30), channel_id=1, source_target_pairs={{0,2},{1,3},{2,0},{3,1},{4,6},{5,7},{6,4},{7,5},{8,10},{9,11},{10,... | collective-permute-start | bytes 393224 | tf_op jit(solution)/shard_map/ppermute | solution.py:18
  130.6 1.7 %collective-permute-start.31 = (f32[256,128]{1,0:T(8,128)S(1)}, f32[256,128]{1,0:T(8,128)S(1)}, u32[]{:S(2)}, u32[]{:S(2)}) collective-permute-start(f32[256,128]{1,0:T(8,128)S(1)} %get-tuple-element.29), channel_id=1, source_target_pairs={{0,3},{1,2},{2,1},{3,0},{4,7},{5,6},{6,5},{7,4},{8,11},{9,10},{10,... | collective-permute-start | bytes 393224 | tf_op jit(solution)/shard_map/ppermute | solution.py:18
  132.3 1.7 %collective-permute-done.30 = f32[256,128]{1,0:T(8,128)S(1)} collective-permute-done((f32[256,128]{1,0:T(8,128)S(1)}, f32[256,128]{1,0:T(8,128)S(1)}, u32[]{:S(2)}, u32[]{:S(2)}) %collective-permute-start.30) | collective-permute-done | bytes 131104 | tf_op jit(solution)/shard_map/ppermute | solution.py:18
  134.0 2.2 %collective-permute-done.31 = f32[256,128]{1,0:T(8,128)S(1)} collective-permute-done((f32[256,128]{1,0:T(8,128)S(1)}, f32[256,128]{1,0:T(8,128)S(1)}, u32[]{:S(2)}, u32[]{:S(2)}) %collective-permute-start.31) | collective-permute-done | bytes 131104 | tf_op jit(solution)/shard_map/ppermute | solution.py:18
  (99 shorter events, 24.7 us)
Async XLA Ops:
  0.7 13.3 %collective-permute-start = (f32[256,128]{1,0:T(8,128)}, f32[256,128]{1,0:T(8,128)S(1)}, u32[]{:S(2)}, u32[]{:S(2)}) collective-permute-start(f32[256,128]{1,0:T(8,128)} %param.11), channel_id=1, source_target_pairs={{0,3},{1,2},{2,1},{3,0},{4,7},{5,6},{6,5},{7,4},{8,11},{9,10},{10,... | collective-permute-start | bytes 393224 | tf_op jit(solution)/shard_map/ppermute | solution.py:18
  3.1 10.8 %collective-permute-start.1 = (f32[256,128]{1,0:T(8,128)}, f32[256,128]{1,0:T(8,128)S(1)}, u32[]{:S(2)}, u32[]{:S(2)}) collective-permute-start(f32[256,128]{1,0:T(8,128)} %param.11), channel_id=1, source_target_pairs={{0,2},{1,3},{2,0},{3,1},{4,6},{5,7},{6,4},{7,5},{8,10},{9,11},{10,... | collective-permute-start | bytes 393224 | tf_op jit(solution)/shard_map/ppermute | solution.py:18
  3.8 10.2 %collective-permute-start.2 = (f32[256,128]{1,0:T(8,128)}, f32[256,128]{1,0:T(8,128)S(1)}, u32[]{:S(2)}, u32[]{:S(2)}) collective-permute-start(f32[256,128]{1,0:T(8,128)} %param.11), channel_id=1, source_target_pairs={{0,1},{1,0},{2,3},{3,2},{4,5},{5,4},{6,7},{7,6},{8,9},{9,8},{10,11... | collective-permute-start | bytes 393224 | tf_op jit(solution)/shard_map/ppermute | solution.py:18
  5.4 33.9 %collective-permute-start.19 = (f32[64,512]{1,0:T(8,128)}, f32[64,512]{1,0:T(8,128)}, u32[]{:S(2)}, u32[]{:S(2)}) collective-permute-start(f32[64,512]{1,0:T(8,128)} %slice_bitcast_fusion.1), channel_id=1, source_target_pairs={{0,12},{4,8},{8,4},{12,0},{16,28},{20,24},{24,20},{28,16},{1,13},{... | collective-permute-start | bytes 393224 | tf_op jit(solution)/shard_map/ppermute | solution.py:18
  14.9 30.9 %collective-permute-start.3 = (f32[256,640]{1,0:T(8,128)S(1)}, f32[256,640]{1,0:T(8,128)S(1)}, u32[]{:S(2)}, u32[]{:S(2)}) collective-permute-start(f32[256,640]{1,0:T(8,128)S(1)} %constant_dynamic-update-slice_fusion.refs_7_), channel_id=1, source_target_pairs={{0,8},{4,12},{8,16},{12,20},{16,24},{20,28},{1,9},{5,13},{9,17},{1... | collective-permute-start | bytes 1966088 | tf_op jit(solution)/shard_map/ppermute | solution.py:24
  17.3 31.4 %collective-permute-start.4 = (f32[256,640]{1,0:T(8,128)S(1)}, f32[256,640]{1,0:T(8,128)S(1)}, u32[]{:S(2)}, u32[]{:S(2)}) collective-permute-start(f32[256,640]{1,0:T(8,128)S(1)} %constant_dynamic-update-slice_fusion.refs_7_), channel_id=1, source_target_pairs={{0,4},{4,8},{8,12},{12,16},{16,20},{20,24},{24,28},{1,5},{5,9},{9,... | collective-permute-start | bytes 1966088 | tf_op jit(solution)/shard_map/ppermute | solution.py:24
  19.6 34.0 %collective-permute-start.5 = (f32[256,640]{1,0:T(8,128)S(1)}, f32[256,640]{1,0:T(8,128)}, u32[]{:S(2)}, u32[]{:S(2)}) collective-permute-start(f32[256,640]{1,0:T(8,128)S(1)} %constant_dynamic-update-slice_fusion.refs_7_), channel_id=1, source_target_pairs={{4,0},{8,4},{12,8},{16,12},{20,16},{24,20},{28,24},{5,1},{9,5},{13... | collective-permute-start | bytes 1966088 | tf_op jit(solution)/shard_map/ppermute | solution.py:24
  20.9 40.9 %collective-permute-start.6 = (f32[256,640]{1,0:T(8,128)S(1)}, f32[256,640]{1,0:T(8,128)}, u32[]{:S(2)}, u32[]{:S(2)}) collective-permute-start(f32[256,640]{1,0:T(8,128)S(1)} %constant_dynamic-update-slice_fusion.refs_7_), channel_id=1, source_target_pairs={{8,0},{12,4},{16,8},{20,12},{24,16},{28,20},{9,1},{13,5},{17,9},{2... | collective-permute-start | bytes 1966088 | tf_op jit(solution)/shard_map/ppermute | solution.py:24
  39.2 35.2 %collective-permute-start.20 = (f32[64,512]{1,0:T(8,128)}, f32[64,512]{1,0:T(8,128)S(1)}, u32[]{:S(2)}, u32[]{:S(2)}) collective-permute-start(f32[64,512]{1,0:T(8,128)} %slice_bitcast_fusion.1), channel_id=1, source_target_pairs={{0,8},{4,12},{8,0},{12,4},{16,24},{20,28},{24,16},{28,20},{1,9},{5... | collective-permute-start | bytes 393224 | tf_op jit(solution)/shard_map/ppermute | solution.py:18
  45.8 28.8 %collective-permute-start.21 = (f32[64,512]{1,0:T(8,128)}, f32[64,512]{1,0:T(8,128)S(1)}, u32[]{:S(2)}, u32[]{:S(2)}) collective-permute-start(f32[64,512]{1,0:T(8,128)} %slice_bitcast_fusion.1), channel_id=1, source_target_pairs={{0,4},{4,0},{8,12},{12,8},{16,20},{20,16},{24,28},{28,24},{1,5},{5... | collective-permute-start | bytes 393224 | tf_op jit(solution)/shard_map/ppermute | solution.py:18
  48.7 27.1 %collective-permute-start.16 = (f32[256,256]{1,0:T(8,128)}, f32[256,256]{1,0:T(8,128)S(1)}, u32[]{:S(2)}, u32[]{:S(2)}) collective-permute-start(f32[256,256]{1,0:T(8,128)} %slice_bitcast_fusion), channel_id=1, source_target_pairs={{0,12},{4,8},{8,4},{12,0},{16,28},{20,24},{24,20},{28,16},{1,13},{... | collective-permute-start | bytes 786440 | tf_op jit(solution)/shard_map/ppermute | solution.py:18
  53.5 22.2 %collective-permute-start.17 = (f32[256,256]{1,0:T(8,128)}, f32[256,256]{1,0:T(8,128)S(1)}, u32[]{:S(2)}, u32[]{:S(2)}) collective-permute-start(f32[256,256]{1,0:T(8,128)} %slice_bitcast_fusion), channel_id=1, source_target_pairs={{0,8},{4,12},{8,0},{12,4},{16,24},{20,28},{24,16},{28,20},{1,9},{5... | collective-permute-start | bytes 786440 | tf_op jit(solution)/shard_map/ppermute | solution.py:18
  61.8 14.0 %collective-permute-start.18 = (f32[256,256]{1,0:T(8,128)}, f32[256,256]{1,0:T(8,128)S(1)}, u32[]{:S(2)}, u32[]{:S(2)}) collective-permute-start(f32[256,256]{1,0:T(8,128)} %slice_bitcast_fusion), channel_id=1, source_target_pairs={{0,4},{4,0},{8,12},{12,8},{16,20},{20,16},{24,28},{28,24},{1,5},{5... | collective-permute-start | bytes 786440 | tf_op jit(solution)/shard_map/ppermute | solution.py:18
  74.5 2.0 %collective-permute-start.8 = (f32[1024,128]{1,0:T(8,128)S(1)}, f32[1024,128]{1,0:T(8,128)S(1)}, u32[]{:S(2)}, u32[]{:S(2)}) collective-permute-start(f32[1024,128]{1,0:T(8,128)S(1)} %get-tuple-element.11), channel_id=1, source_target_pairs={{0,1},{1,0},{2,3},{3,2},{4,5},{5,4},{6,7},{7,6},{8,9},{9,8},{10,11... | collective-permute-start | bytes 1572872 | tf_op jit(solution)/shard_map/ppermute | solution.py:18
  75.9 5.2 %collective-permute-start.7 = (f32[1024,128]{1,0:T(8,128)S(1)}, f32[1024,128]{1,0:T(8,128)S(1)}, u32[]{:S(2)}, u32[]{:S(2)}) collective-permute-start(f32[1024,128]{1,0:T(8,128)S(1)} %get-tuple-element.9), channel_id=1, source_target_pairs={{0,1},{1,0},{2,3},{3,2},{4,5},{5,4},{6,7},{7,6},{8,9},{9,8},{10,11... | collective-permute-start | bytes 1572872 | tf_op jit(solution)/shard_map/ppermute | solution.py:18
  76.5 14.0 %collective-permute-start.9 = (f32[1024,128]{1,0:T(8,128)S(1)}, f32[1024,128]{1,0:T(8,128)S(1)}, u32[]{:S(2)}, u32[]{:S(2)}) collective-permute-start(f32[1024,128]{1,0:T(8,128)S(1)} %add.95), channel_id=1, source_target_pairs={{0,2},{1,3},{2,0},{3,1},{4,6},{5,7},{6,4},{7,5},{8,10},{9,11},{10,... | collective-permute-start | bytes 1572872 | tf_op jit(solution)/shard_map/ppermute | solution.py:18
  91.3 6.1 %collective-permute-start.13 = (f32[256,128]{1,0:T(8,128)S(1)}, f32[256,128]{1,0:T(8,128)S(1)}, u32[]{:S(2)}, u32[]{:S(2)}) collective-permute-start(f32[256,128]{1,0:T(8,128)S(1)} %fusion.58), channel_id=1, source_target_pairs={{0,4},{4,0},{8,12},{12,8},{16,20},{20,16},{24,28},{28,24},{1,5},{5... | collective-permute-start | bytes 393224 | tf_op jit(solution)/shard_map/ppermute | solution.py:18
  93.3 5.8 %collective-permute-start.14 = (f32[256,128]{1,0:T(8,128)S(1)}, f32[256,128]{1,0:T(8,128)S(1)}, u32[]{:S(2)}, u32[]{:S(2)}) collective-permute-start(f32[256,128]{1,0:T(8,128)S(1)} %fusion.58), channel_id=1, source_target_pairs={{0,8},{4,12},{8,0},{12,4},{16,24},{20,28},{24,16},{28,20},{1,9},{5... | collective-permute-start | bytes 393224 | tf_op jit(solution)/shard_map/ppermute | solution.py:18
  93.4 7.0 %collective-permute-start.15 = (f32[256,128]{1,0:T(8,128)S(1)}, f32[256,128]{1,0:T(8,128)S(1)}, u32[]{:S(2)}, u32[]{:S(2)}) collective-permute-start(f32[256,128]{1,0:T(8,128)S(1)} %fusion.58), channel_id=1, source_target_pairs={{0,12},{4,8},{8,4},{12,0},{16,28},{20,24},{24,20},{28,16},{1,13},{... | collective-permute-start | bytes 393224 | tf_op jit(solution)/shard_map/ppermute | solution.py:18
  101.4 6.1 %collective-permute-start.22 = (f32[256,128]{0,1:T(8,128)S(1)}, f32[256,128]{0,1:T(8,128)S(1)}, u32[]{:S(2)}, u32[]{:S(2)}) collective-permute-start(f32[256,128]{0,1:T(8,128)S(1)} %convolution_bitcast_fusion), channel_id=1, source_target_pairs={{0,4},{4,0},{8,12},{12,8},{16,20},{20,16},{24,28},{28,24},{1,5},{5... | collective-permute-start | bytes 393224 | tf_op jit(solution)/shard_map/ppermute | solution.py:18
  103.1 5.0 %collective-permute-start.23 = (f32[256,128]{0,1:T(8,128)S(1)}, f32[256,128]{0,1:T(8,128)S(1)}, u32[]{:S(2)}, u32[]{:S(2)}) collective-permute-start(f32[256,128]{0,1:T(8,128)S(1)} %convolution_bitcast_fusion), channel_id=1, source_target_pairs={{0,8},{4,12},{8,0},{12,4},{16,24},{20,28},{24,16},{28,20},{1,9},{5... | collective-permute-start | bytes 393224 | tf_op jit(solution)/shard_map/ppermute | solution.py:18
  103.4 5.9 %collective-permute-start.24 = (f32[256,128]{0,1:T(8,128)S(1)}, f32[256,128]{0,1:T(8,128)S(1)}, u32[]{:S(2)}, u32[]{:S(2)}) collective-permute-start(f32[256,128]{0,1:T(8,128)S(1)} %convolution_bitcast_fusion), channel_id=1, source_target_pairs={{0,12},{4,8},{8,4},{12,0},{16,28},{20,24},{24,20},{28,16},{1,13},{... | collective-permute-start | bytes 393224 | tf_op jit(solution)/shard_map/ppermute | solution.py:18
  109.3 5.9 %collective-permute-start.25 = (f32[256,128]{0,1:T(8,128)S(1)}, f32[256,128]{0,1:T(8,128)S(1)}, u32[]{:S(2)}, u32[]{:S(2)}) collective-permute-start(f32[256,128]{0,1:T(8,128)S(1)} %add_add_fusion.1), channel_id=1, source_target_pairs={{0,16},{4,20},{8,24},{12,28},{16,0},{20,4},{24,8},{28,12},{1,17},{... | collective-permute-start | bytes 393224 | tf_op jit(solution)/shard_map/ppermute | solution.py:18
  113.5 10.7 %collective-permute-start.10 = (f32[256,128]{1,0:T(8,128)S(1)}, f32[256,128]{1,0:T(8,128)S(1)}, u32[]{:S(2)}, u32[]{:S(2)}) collective-permute-start(f32[256,128]{1,0:T(8,128)S(1)} %get-tuple-element.38), channel_id=1, source_target_pairs={{0,1},{1,0},{2,3},{3,2},{4,5},{5,4},{6,7},{7,6},{8,9},{9,8},{10,11... | collective-permute-start | bytes 393224 | tf_op jit(solution)/shard_map/ppermute | solution.py:18
  115.9 8.3 %collective-permute-start.26 = (f32[256,128]{0,1:T(8,128)S(1)}, f32[256,128]{0,1:T(8,128)S(1)}, u32[]{:S(2)}, u32[]{:S(2)}) collective-permute-start(f32[256,128]{0,1:T(8,128)S(1)} %convolution_subtract_fusion.1), channel_id=1, source_target_pairs={{0,12},{4,8},{8,4},{12,0},{16,28},{20,24},{24,20},{28,16},{1,13},{... | collective-permute-start | bytes 393224 | tf_op jit(solution)/shard_map/ppermute | solution.py:18
  117.6 7.1 %collective-permute-start.27 = (f32[256,128]{0,1:T(8,128)S(1)}, f32[256,128]{0,1:T(8,128)S(1)}, u32[]{:S(2)}, u32[]{:S(2)}) collective-permute-start(f32[256,128]{0,1:T(8,128)S(1)} %convolution_subtract_fusion.1), channel_id=1, source_target_pairs={{0,8},{4,12},{8,0},{12,4},{16,24},{20,28},{24,16},{28,20},{1,9},{5... | collective-permute-start | bytes 393224 | tf_op jit(solution)/shard_map/ppermute | solution.py:18
  120.4 5.0 %collective-permute-start.28 = (f32[256,128]{0,1:T(8,128)S(1)}, f32[256,128]{0,1:T(8,128)S(1)}, u32[]{:S(2)}, u32[]{:S(2)}) collective-permute-start(f32[256,128]{0,1:T(8,128)S(1)} %convolution_subtract_fusion.1), channel_id=1, source_target_pairs={{0,4},{4,0},{8,12},{12,8},{16,20},{20,16},{24,28},{28,24},{1,5},{5... | collective-permute-start | bytes 393224 | tf_op jit(solution)/shard_map/ppermute | solution.py:18
  122.5 5.5 %collective-permute-start.11 = (f32[256,128]{1,0:T(8,128)S(1)}, f32[256,128]{1,0:T(8,128)S(1)}, u32[]{:S(2)}, u32[]{:S(2)}) collective-permute-start(f32[256,128]{1,0:T(8,128)S(1)} %get-tuple-element.37), channel_id=1, source_target_pairs={{0,2},{1,3},{2,0},{3,1},{4,6},{5,7},{6,4},{7,5},{8,10},{9,11},{10,... | collective-permute-start | bytes 393224 | tf_op jit(solution)/shard_map/ppermute | solution.py:18
  124.2 6.3 %collective-permute-start.12 = (f32[256,128]{1,0:T(8,128)S(1)}, f32[256,128]{1,0:T(8,128)S(1)}, u32[]{:S(2)}, u32[]{:S(2)}) collective-permute-start(f32[256,128]{1,0:T(8,128)S(1)} %get-tuple-element.36), channel_id=1, source_target_pairs={{0,3},{1,2},{2,1},{3,0},{4,7},{5,6},{6,5},{7,4},{8,11},{9,10},{10,... | collective-permute-start | bytes 393224 | tf_op jit(solution)/shard_map/ppermute | solution.py:18
  126.1 6.2 %collective-permute-start.29 = (f32[256,128]{1,0:T(8,128)S(1)}, f32[256,128]{1,0:T(8,128)S(1)}, u32[]{:S(2)}, u32[]{:S(2)}) collective-permute-start(f32[256,128]{1,0:T(8,128)S(1)} %get-tuple-element.31), channel_id=1, source_target_pairs={{0,1},{1,0},{2,3},{3,2},{4,5},{5,4},{6,7},{7,6},{8,9},{9,8},{10,11... | collective-permute-start | bytes 393224 | tf_op jit(solution)/shard_map/ppermute | solution.py:18
  128.0 6.0 %collective-permute-start.30 = (f32[256,128]{1,0:T(8,128)S(1)}, f32[256,128]{1,0:T(8,128)S(1)}, u32[]{:S(2)}, u32[]{:S(2)}) collective-permute-start(f32[256,128]{1,0:T(8,128)S(1)} %get-tuple-element.30), channel_id=1, source_target_pairs={{0,2},{1,3},{2,0},{3,1},{4,6},{5,7},{6,4},{7,5},{8,10},{9,11},{10,... | collective-permute-start | bytes 393224 | tf_op jit(solution)/shard_map/ppermute | solution.py:18
  130.6 5.6 %collective-permute-start.31 = (f32[256,128]{1,0:T(8,128)S(1)}, f32[256,128]{1,0:T(8,128)S(1)}, u32[]{:S(2)}, u32[]{:S(2)}) collective-permute-start(f32[256,128]{1,0:T(8,128)S(1)} %get-tuple-element.29), channel_id=1, source_target_pairs={{0,3},{1,2},{2,1},{3,0},{4,7},{5,6},{6,5},{7,4},{8,11},{9,10},{10,... | collective-permute-start | bytes 393224 | tf_op jit(solution)/shard_map/ppermute | solution.py:18
  (13 other events, 233.8 us)
